TPU v7x, 256 devices: a whole 4x4x8 slice. The times are simulated.
256 devices in a mesh: view: 2 (over y_lo), tm: 8 (over x, core), head: 16 (over z, y_hi).
Axes of the slice: x: 4, y: 4 (y_hi: 2, y_lo: 2; y = y_hi * 2 + y_lo), z: 8, core: 2. Of those that a mesh axis runs over, the one named last changes fastest.
Arguments:
- tokens: bfloat16 [4, 1024, 5120], P('view', ('tm', 'head')), may hold values from -16 to 16, as said below
- query_weight: bfloat16 [5120, 4096], P(('view', 'tm'), 'head'), as said below
- key_weight: bfloat16 [5120, 4096], P(('view', 'tm'), 'head'), as said below
- value_weight: bfloat16 [5120, 4096], P(('view', 'tm'), 'head'), may hold values from -0.078125 to 0.078125
- out_grad: bfloat16 [4, 1024, 4096], P('view', 'tm', 'head'), may hold values from -6 to 6
- pairs: int32 [5, 2], replicated, may hold values from 0 to 3, as said below
- block_masks: int32 [4, 16], replicated, may hold values from 0 to 1, as said below
Outputs:
- attended: bfloat16 [4, 1024, 4096], P('view', 'tm', 'head')
- token_grad: bfloat16 [4, 1024, 5120], P('view', ('tm', 'head'))
- query_weight_grad: bfloat16 [5120, 4096], P(('view', 'tm'), 'head')
- key_weight_grad: bfloat16 [5120, 4096], P(('view', 'tm'), 'head')
- value_weight_grad: bfloat16 [5120, 4096], P(('view', 'tm'), 'head')
Inputs may be any that keep to these rules, and one draw needn't show every extreme that they name: `tokens`: row scales may differ from token to token. `query_weight`: entries of order 5120 ** -0.5. `key_weight`: entries of order 5120 ** -0.5. `pairs`: each row (i, j) has i < j; rows are distinct; every camera appears in two or more rows. `block_masks`: every camera has at least one block equal to 1.
All inputs are finite; a program needn't handle non-finite values.
Results may differ from a plain program's by a relative error of at most 0.04.
Values may be sent and summed in bfloat16 or wider, within the bound.
A program may use at most 128 MiB of HBM per device.

v0:
```python
import math

import jax
import jax.numpy as jnp
from jax import lax
from jax.sharding import PartitionSpec as P

HEAD_SIZE = 128


big_negative = -1e30


def linked_table(pairs, cameras):
    ids = jnp.arange(cameras, dtype=jnp.int32)
    first = pairs[:, 0][:, None, None]
    second = pairs[:, 1][:, None, None]
    row_ids = ids[None, :, None]
    col_ids = ids[None, None, :]
    hits = (first == row_ids) & (second == col_ids) | (first == col_ids) & (second == row_ids)
    return jnp.max(hits.astype(jnp.int32), axis=0)


def open_table(block_masks, camera, block):
    per_camera = block_masks.shape[1]
    flat_index = camera * per_camera + block
    slots = jnp.arange(block_masks.shape[0] * per_camera, dtype=jnp.int32)
    hits = (flat_index[:, None] == slots[None, :]).astype(jnp.int32)
    return jnp.sum(hits * block_masks.reshape(1, -1), axis=1)


def allowed_rows(linked, query_cams, key_cams, key_open):
    ids = jnp.arange(linked.shape[0], dtype=jnp.int32)
    query_hot = (query_cams[:, None] == ids[None, :]).astype(jnp.int32)
    key_hot = (key_cams[:, None] == ids[None, :]).astype(jnp.int32)
    row_links = jnp.sum(query_hot[:, :, None] * linked[None, :, :], axis=1)
    pair_links = jnp.sum(row_links[:, None, :] * key_hot[None, :, :], axis=2)
    return pair_links * key_open[None, :] > 0


def key_layout(shards, cam_dev, tok_dev, n_time, span):
    count = shards.shape[0]
    camera = (shards // n_time)[:, None, None] * cam_dev + jnp.arange(cam_dev, dtype=jnp.int32)[
        None, :, None
    ]
    position = (shards % n_time)[:, None, None] * tok_dev + jnp.arange(tok_dev, dtype=jnp.int32)[
        None, None, :
    ]
    camera = jnp.broadcast_to(camera, (count, cam_dev, tok_dev)).reshape(-1)
    block = jnp.broadcast_to(position // span, (count, cam_dev, tok_dev)).reshape(-1)
    return (camera, block)


def weight_term(flat, grads):
    return lax.dot_general(
        flat, grads, (((0,), (0,)), ((), ())), preferred_element_type=jnp.float32
    )


def back_project(grad, weight):
    return lax.dot_general(
        grad, weight, (((1,), (1,)), ((), ())), preferred_element_type=jnp.float32
    )


def on_device(tokens, query_weight, key_weight, value_weight, out_grad, pairs, block_masks):
    cam_dev = tokens.shape[0]
    n_view = lax.axis_size("view")
    n_time = lax.axis_size("tm")
    n_shards = n_view * n_time
    n_blocks = n_shards // 2
    width = query_weight.shape[1]
    heads = width // HEAD_SIZE
    scale = 1.0 / math.sqrt(HEAD_SIZE)
    full = lax.all_gather(tokens, "head", axis=1, tiled=True)
    tok_dev = full.shape[1]
    rows = cam_dev * tok_dev
    span = tok_dev // 2
    flat = full.reshape(rows, full.shape[2])
    w_query, w_key, w_value = (
        lax.all_gather(query_weight, ("view", "tm"), axis=0, tiled=True),
        lax.all_gather(key_weight, ("view", "tm"), axis=0, tiled=True),
        lax.all_gather(value_weight, ("view", "tm"), axis=0, tiled=True),
    )
    query = jnp.dot(flat, w_query, preferred_element_type=jnp.float32).astype(jnp.bfloat16)
    key = jnp.dot(flat, w_key, preferred_element_type=jnp.float32).astype(jnp.bfloat16)
    value = jnp.dot(flat, w_value, preferred_element_type=jnp.float32).astype(jnp.bfloat16)
    linked = linked_table(pairs, cam_dev * n_view)
    local_cams = lax.axis_index("view") * cam_dev + jnp.arange(cam_dev, dtype=jnp.int32)
    key_all, value_all = (
        lax.all_gather(key.reshape(1, rows, width), ("view", "tm"), axis=0, tiled=True),
        lax.all_gather(value.reshape(1, rows, width), ("view", "tm"), axis=0, tiled=True),
    )
    key_blocks = key_all.reshape(n_blocks, 2 * rows, heads, HEAD_SIZE)
    value_blocks = value_all.reshape(n_blocks, 2 * rows, heads, HEAD_SIZE)
    all_cams, all_spans = key_layout(
        jnp.arange(n_shards, dtype=jnp.int32), cam_dev, tok_dev, n_time, span
    )
    allowed = allowed_rows(
        linked, local_cams, all_cams, open_table(block_masks, all_cams, all_spans)
    )
    allowed_blocks = allowed.reshape(cam_dev, n_blocks, 2 * rows).transpose(1, 0, 2)
    query_heads = query.reshape(cam_dev, tok_dev, heads, HEAD_SIZE)

    def scores(block_keys, mask):
        raw = (
            jnp.einsum(
                "ctae,kae->ctak", query_heads, block_keys, preferred_element_type=jnp.float32
            )
            * scale
        )
        return (raw, mask[:, None, None, :])

    def max_sum(carry, inputs):
        running_max, running_sum = carry
        block_keys, mask = inputs
        raw, open_mask = scores(block_keys, mask)
        block_max = jnp.max(jnp.where(open_mask, raw, big_negative), axis=3)
        new_max = jnp.maximum(running_max, block_max)
        shifted = jnp.exp(jnp.where(open_mask, raw - new_max[..., None], -jnp.inf))
        new_sum = running_sum * jnp.exp(running_max - new_max) + jnp.sum(shifted, axis=3)
        return ((new_max, new_sum), None)

    start_max = jnp.full((cam_dev, tok_dev, heads), big_negative, jnp.float32)
    start_sum = jnp.zeros((cam_dev, tok_dev, heads), jnp.float32)
    (row_max, row_sum), _ = lax.scan(max_sum, (start_max, start_sum), (key_blocks, allowed_blocks))
    log_total = row_max + jnp.log(row_sum)

    def weigh(block_keys, mask):
        raw, open_mask = scores(block_keys, mask)
        return jnp.exp(jnp.where(open_mask, raw - log_total[..., None], -jnp.inf))

    def mix_values(acc, inputs):
        block_keys, block_values, mask = inputs
        probs = weigh(block_keys, mask).astype(jnp.bfloat16)
        return (
            acc
            + jnp.einsum("ctak,kae->ctae", probs, block_values, preferred_element_type=jnp.float32),
            None,
        )

    head_zeros = jnp.zeros((cam_dev, tok_dev, heads, HEAD_SIZE), jnp.float32)
    mixed, _ = lax.scan(mix_values, head_zeros, (key_blocks, value_blocks, allowed_blocks))
    attended_heads = mixed.astype(jnp.bfloat16)
    attended = attended_heads.reshape(cam_dev, tok_dev, width)
    grad_heads = out_grad.reshape(cam_dev, tok_dev, heads, HEAD_SIZE)
    delta = jnp.sum(grad_heads.astype(jnp.float32) * attended_heads.astype(jnp.float32), axis=3)

    def score_grads(block_keys, block_values, mask):
        weights = weigh(block_keys, mask)
        dprob = jnp.einsum(
            "ctae,kae->ctak", grad_heads, block_values, preferred_element_type=jnp.float32
        )
        dscore = (weights * (dprob - delta[..., None]) * scale).astype(jnp.bfloat16)
        return (weights.astype(jnp.bfloat16), dscore)

    def back_step(acc, inputs):
        block_keys, block_values, mask = inputs
        probs, dscore = score_grads(block_keys, block_values, mask)
        acc = acc + jnp.einsum(
            "ctak,kae->ctae", dscore, block_keys, preferred_element_type=jnp.float32
        )
        key_term = jnp.einsum(
            "ctak,ctae->kae", dscore, query_heads, preferred_element_type=jnp.float32
        )
        value_term = jnp.einsum(
            "ctak,ctae->kae", probs, grad_heads, preferred_element_type=jnp.float32
        )
        term = jnp.concatenate((key_term.reshape(-1, width), value_term.reshape(-1, width)), axis=1)
        return (acc, term)

    query_acc, key_terms = lax.scan(
        back_step, head_zeros, (key_blocks, value_blocks, allowed_blocks)
    )
    query_grad = query_acc.astype(jnp.bfloat16).reshape(rows, width)
    summed = lax.psum_scatter(
        key_terms.reshape(n_shards * rows, 2 * width).astype(jnp.bfloat16),
        ("view", "tm"),
        scatter_dimension=0,
        tiled=True,
    ).astype(jnp.float32)
    key_grad = summed[:, :width].astype(jnp.bfloat16)
    value_grad = summed[:, width:].astype(jnp.bfloat16)
    input_term = (
        back_project(query_grad, w_query)
        + back_project(key_grad, w_key)
        + back_project(value_grad, w_value)
    )
    token_grad = lax.psum_scatter(
        input_term.reshape(cam_dev, tok_dev, -1).astype(jnp.bfloat16),
        "head",
        scatter_dimension=1,
        tiled=True,
    )
    stacked = jnp.concatenate((query_grad, key_grad, value_grad), axis=1)
    grads = lax.psum_scatter(
        weight_term(flat, stacked).astype(jnp.bfloat16),
        ("view", "tm"),
        scatter_dimension=0,
        tiled=True,
    )
    query_weight_grad = grads[:, :width]
    key_weight_grad = grads[:, width : 2 * width]
    value_weight_grad = grads[:, 2 * width :]
    return (attended, token_grad, query_weight_grad, key_weight_grad, value_weight_grad)


def solution(mesh):
    return jax.shard_map(
        on_device,
        mesh=mesh,
        in_specs=(
            P("view", ("tm", "head"), None),
            P(("view", "tm"), "head"),
            P(("view", "tm"), "head"),
            P(("view", "tm"), "head"),
            P("view", "tm", "head"),
            P(),
            P(),
        ),
        out_specs=(
            P("view", "tm", "head"),
            P("view", ("tm", "head"), None),
            P(("view", "tm"), "head"),
            P(("view", "tm"), "head"),
            P(("view", "tm"), "head"),
        ),
        check_vma=False,
    )
```

profile of v0, /device:TPU:2, one launch (start us, length us, event | category | flops | bytes accessed | tf_op | source)
XLA Modules:
  0.0 744.1 jit_solution(13030034438299127346)
XLA Ops:
  10.8 92.1 %all-gather.9.cloned.1.call-done = bf16[2,128,5120]{2,1,0:T(8,128)(2,1)} async-done(((bf16[2,8,5120]{2,1,0:T(8,128)(2,1)}), bf16[2,128,5120]{2,1,0:T(8,128)(2,1)}) %all-gather.9.cloned.1.call-update) | async-done | bytes 2621456 | tf_op jit(solution)/shard_map/all_gather | solution.py:75
  103.0 35.7 %all-gather.13.cloned.1.call-done = bf16[5120,256]{1,0:T(8,128)(2,1)} async-done(((bf16[320,256]{1,0:T(8,128)(2,1)}), bf16[5120,256]{1,0:T(8,128)(2,1)}) %all-gather.13.cloned.1.call-update) | async-done | bytes 2621456 | tf_op jit(solution)/shard_map/all_gather | solution.py:82
  138.7 4.2 convolution_convert_fusion.2
  144.2 33.8 %all-gather.15.cloned.1.call-done = bf16[5120,256]{1,0:T(8,128)(2,1)} async-done(((bf16[320,256]{1,0:T(8,128)(2,1)}), bf16[5120,256]{1,0:T(8,128)(2,1)}) %all-gather.15.cloned.1.call-update) | async-done | bytes 2621456 | tf_op jit(solution)/shard_map/all_gather | solution.py:81
  178.1 2.6 convolution_convert_fusion.1
  181.5 35.8 %all-gather.11.cloned.1.call-done = bf16[5120,256]{1,0:T(8,128)(2,1)} async-done(((bf16[320,256]{1,0:T(8,128)(2,1)}), bf16[5120,256]{1,0:T(8,128)(2,1)}) %all-gather.11.cloned.1.call-update) | async-done | bytes 2621456 | tf_op jit(solution)/shard_map/all_gather | solution.py:83
  217.3 3.2 convolution_convert_fusion.3
  220.6 35.4 %all-gather.19.cloned.1.call-done = bf16[4096,256]{1,0:T(8,128)(2,1)} async-done(((bf16[256,256]{1,0:T(8,128)(2,1)}), bf16[4096,256]{1,0:T(8,128)(2,1)}) %all-gather.19.cloned.1.call-update) | async-done | bytes 2097168 | tf_op jit(solution)/shard_map/all_gather | solution.py:91
  256.0 4.0 reshape.336
  260.0 2.0 copy.112
  262.0 7.2 while.37
  270.5 24.5 %all-gather.17.cloned.1.call-done = bf16[4096,256]{1,0:T(8,128)(2,1)} async-done(((bf16[256,256]{1,0:T(8,128)(2,1)}), bf16[4096,256]{1,0:T(8,128)(2,1)}) %all-gather.17.cloned.1.call-update) | async-done | bytes 2097168 | tf_op jit(solution)/shard_map/all_gather | solution.py:92
  294.9 2.5 reshape.333
  297.5 21.3 %while.38 = (s32[]{:T(128)}, f32[2,128,2,128]{1,3,0,2:T(8,128)}, bf16[8,512,2,128]{3,2,1,0:T(2,128)(2,1)S(1)}, pred[8,2,512]{2,1,0:T(4,128)(4,1)S(1)}, bf16[8,51...) while((s32[]{:T(128)}, f32[2,128,2,128]{1,3,0,2:T(8,128)}, ...), condition=%wide.region_9.10_spmd.clone, body=%wide.region_8.9_spmd.clone.sunk | while | flops 135397376 | bytes 2233467 | solution.py:143
  297.9 2.2 fusion.108
  300.5 2.3 fusion.108
  303.1 2.3 fusion.108
  305.8 2.3 fusion.108
  308.5 2.3 fusion.108
  311.2 2.3 fusion.108
  313.8 2.3 fusion.108
  316.5 2.3 fusion.108
  318.8 1.6 multiply_reduce_fusion
  321.1 51.7 %while.39 = (s32[]{:T(128)}, f32[2,128,2,128]{1,3,0,2:T(8,128)S(1)}, bf16[8,512,512]{2,1,0:T(8,128)(2,1)}, bf16[8,512,2,128]{3,1,2,0:T(8,128)(2,1)}, pred[8,2,51...) while((s32[]{:T(128)}, ...), condition=%wide.region_12.13_spmd.clone, body=%wide.region_11.12_spmd.clone.sunk | while | flops 338821120 | bytes 10755227 | solution.py:172
  321.2 1.4 fusion.118
  323.9 1.3 fusion.120
  325.2 1.2 fusion.122
  327.7 1.4 fusion.118
  329.1 1.0 fusion.119
  330.4 1.3 fusion.120
  331.6 1.2 fusion.122
  334.1 1.4 fusion.118
  336.8 1.3 fusion.120
  338.1 1.2 fusion.122
  340.6 1.4 fusion.118
  343.3 1.3 fusion.120
  344.5 1.2 fusion.122
  347.0 1.4 fusion.118
  348.4 1.0 fusion.119
  349.7 1.3 fusion.120
  351.0 1.2 fusion.122
  353.5 1.4 fusion.118
  356.2 1.3 fusion.120
  357.5 1.2 fusion.122
  360.0 1.4 fusion.118
  361.4 1.0 fusion.119
  362.7 1.3 fusion.120
  363.9 1.2 fusion.122
  366.5 1.4 fusion.118
  367.8 1.0 fusion.119
  369.1 1.3 fusion.120
  370.4 1.2 fusion.122
  373.2 5.0 fusion.60
  378.2 60.3 %reduce-scatter.8.cloned.1.call-done = bf16[256,512]{1,0:T(8,128)(2,1)} async-done(((bf16[4096,512]{1,0:T(8,128)(2,1)}), bf16[256,512]{1,0:T(8,128)(2,1)}) %reduce-scatter.8.cloned.1.call-update) | async-done | bytes 262160 | tf_op jit(solution)/shard_map/reduce_scatter | solution.py:176
  438.5 3.6 convolution_add_fusion.1
  443.1 2.7 copy.144
  445.8 2.2 copy.158
  448.0 1.6 copy-done.3
  449.7 5.3 fusion.44
  455.0 10.7 %copy.146 = bf16[5120,768]{1,0:T(8,128)(2,1)} copy(bf16[5120,768]{0,1:T(8,128)(2,1)} %fusion.44) | data formatting | bytes 15728640
  467.3 195.8 %reduce-scatter.10.cloned.1.call-done = bf16[8,10240]{1,0:T(8,128)(2,1)} async-done(((bf16[128,10240]{1,0:T(8,128)(2,1)}), bf16[8,10240]{1,0:T(8,128)(2,1)}) %reduce-scatter.10.cloned.1.call-update) | async-done | bytes 163856
  663.2 1.0 reshape.356
  664.9 70.8 %reduce-scatter.12.cloned.1.call-done = bf16[320,768]{1,0:T(8,128)(2,1)} async-done(((bf16[5120,768]{1,0:T(8,128)(2,1)}), bf16[320,768]{1,0:T(8,128)(2,1)}) %reduce-scatter.12.cloned.1.call-update) | async-done | bytes 491536
  735.7 1.9 fusion.61
  (197 shorter events, 37.4 us)
Async XLA Ops:
  7.2 95.8 %all-gather.9.cloned.1.call-start = ((), (), s32[]{:S(2)}) async-start(), calls=%async_computation.3 | async-start | bytes 2785280 | tf_op jit(solution)/shard_map/all_gather | solution.py:75
  7.9 130.8 %all-gather.13.cloned.1.call-start = ((), (), s32[]{:S(2)}) async-start(), calls=%async_computation.5 | async-start | bytes 2785280 | tf_op jit(solution)/shard_map/all_gather | solution.py:82
  8.6 169.4 %all-gather.15.cloned.1.call-start = ((), (), s32[]{:S(2)}) async-start(), calls=%async_computation.6 | async-start | bytes 2785280 | tf_op jit(solution)/shard_map/all_gather | solution.py:81
  9.4 207.9 %all-gather.11.cloned.1.call-start = ((), (), s32[]{:S(2)}) async-start(), calls=%async_computation.4 | async-start | bytes 2785280 | tf_op jit(solution)/shard_map/all_gather | solution.py:83
  10.0 246.0 %all-gather.19.cloned.1.call-start = ((), (), s32[]{:S(2)}) async-start(), calls=%async_computation.9 | async-start | bytes 2228224 | tf_op jit(solution)/shard_map/all_gather | solution.py:91
  138.7 4.8 copy-start.8
  138.7 5.4 copy-start.7
  138.7 39.4 %copy-start.2 = (bf16[2,128,5120]{2,1,0:T(8,128)(2,1)S(1)}, bf16[2,128,5120]{2,1,0:T(8,128)(2,1)}, u32[]{:S(2)}) copy-start(bf16[2,128,5120]{2,1,0:T(8,128)(2,1)} %all-gather.9.cloned.1.call-done) | copy-start | bytes 7864324
  142.9 152.0 %all-gather.17.cloned.1.call-start = ((), (), s32[]{:S(2)}) async-start(), calls=%async_computation.8 | async-start | bytes 2228224 | tf_op jit(solution)/shard_map/all_gather | solution.py:92
  220.5 218.0 %reduce-scatter.8.cloned.1.call-start = ((), (), s32[]{:S(2)}) async-start(), calls=%async_computation.7 | async-start | bytes 4456448 | tf_op jit(solution)/shard_map/reduce_scatter | solution.py:176
  269.2 1.3 copy-start
  372.7 290.4 %reduce-scatter.10.cloned.1.call-start = ((), (), s32[]{:S(2)}) async-start(), calls=%async_computation.10 | async-start | bytes 2785280
  373.1 65.4 %copy-start.1 = (bf16[5120,256]{1,0:T(8,128)(2,1)S(1)}, bf16[5120,256]{1,0:T(8,128)(2,1)}, u32[]{:S(2)}) copy-start(bf16[5120,256]{1,0:T(8,128)(2,1)} %all-gather.13.cloned.1.call-done) | copy-start | bytes 7864324
  438.5 3.6 copy-start.4
  438.5 3.6 copy-start.5
  447.9 1.7 copy-start.3
  448.0 287.7 %reduce-scatter.12.cloned.1.call-start = ((), (), s32[]{:S(2)}) async-start(), calls=%async_computation.11 | async-start | bytes 8355840
  465.7 0.9 copy-start.6
Sparse Core Ops, SparseCore 0:
  10.6 92.3 all-gather.8
  104.8 33.8 all-gather.12
  140.6 37.4 all-gather.14
  179.8 37.4 all-gather.10
  219.6 36.3 all-gather.18
  258.3 36.6 all-gather.16
  372.9 65.5 reduce-scatter.7
  448.1 215.0 reduce-scatter.9
  665.8 69.8 reduce-scatter.11
where the time goes:
time: 750 us; the launch traced here: 744 us
  waiting for transfers between devices  587 us (78%)
  matrix products  88.6 us (12%)
  local copies, waits for them, and re-layouts  47 us (6%)
  between operations  14.1 us (2%)
    unnamed x11, waiting for transfers between devices  269 us
    all_gather x1, waiting for transfers between devices, on_device(): full = lax.all_gather(tokens, 'head', axis=1, tiled=True)  92.1 us
    reduce_scatter x1, waiting for transfers between devices, on_device(): lax.psum_scatter(key_terms.reshape(n_shards * rows, 2 * width).astype(jnp...  60.3 us
    all_gather x1, waiting for transfers between devices, on_device(): lax.all_gather(value_weight, ('view', 'tm'), axis=0, tiled=True)  35.8 us
    all_gather x1, waiting for transfers between devices, on_device(): lax.all_gather(key_weight, ('view', 'tm'), axis=0, tiled=True)  35.7 us
    all_gather x1, waiting for transfers between devices, on_device(): lax.all_gather(key.reshape(1, rows, width), ('view', 'tm'), axis=0, tiled...  35.4 us
    all_gather x1, waiting for transfers between devices, on_device(): lax.all_gather(query_weight, ('view', 'tm'), axis=0, tiled=True)  33.8 us
    unnamed x32, local copies, waits for them, and re-layouts  24.8 us
  transfers between devices with their start and end apart: 9, of which 9 were waited for; matrix products, arithmetic and copies ran while one was open for 7% of the time, Pallas kernels for 0%

commit v1 on v0

v1 whole, which is shorter than its diff:
```python
import math

import jax
import jax.numpy as jnp
from jax import lax
from jax.experimental import pallas as pl
from jax.experimental.pallas import tpu as pltpu
from jax.sharding import PartitionSpec as P

MESH = pl.DeviceIdType.MESH
F32 = jnp.float32
BF16 = jnp.bfloat16
VMEM_LIMIT = 58 * 1024 * 1024

HALF = 2560
ROWS = 512
SCALE = 1.0 / math.sqrt(128)
CLOSED = -1e30


class Place:
    def __init__(self):
        self.v = lax.axis_index("view")
        self.t = lax.axis_index("tm")
        self.h = lax.axis_index("head")
        v, t, h = self.v, self.t, self.h
        self.x, self.core = t // 2, lax.rem(t, 2)
        self.z, self.y = h // 2, lax.rem(h, 2)
        self.sib_t = t + 1 - 2 * self.core
        other_h = h + 1 - 2 * self.y
        self.V = {"view": 1 - v}
        self.Y = {"head": other_h}
        self.D = {"view": 1 - v, "head": other_h}
        self.ZP = {"head": lax.rem(h + 2, 16)}
        self.ZM = {"head": lax.rem(h + 14, 16)}
        self.XP = {"tm": lax.rem(t + 2, 8)}
        self.XM = {"tm": lax.rem(t + 6, 8)}
        self.S = {"tm": self.sib_t}

    def greet(self):
        bar = pltpu.get_barrier_semaphore()
        peers = (self.V, self.Y, self.D, self.ZP, self.ZM, self.XP, self.XM, self.S)
        for peer in peers:
            pl.semaphore_signal(bar, inc=1, device_id=peer, device_id_type=MESH)
        pl.semaphore_wait(bar, len(peers))


def rcopy(src, dst, ss, rs, dev):
    return pltpu.make_async_remote_copy(
        src_ref=src, dst_ref=dst, send_sem=ss, recv_sem=rs, device_id=dev, device_id_type=MESH
    )


def lanes(start, size):
    return pl.ds(pl.multiple_of(start, 128), size)


class RingGather:
    def __init__(self, pc, at, ss, rs):
        self.pc, self.at, self.ss, self.rs = pc, at, ss, rs
        self.sent = []

    def cp(self, i, t, half, dev):
        ref = self.at(t, half)
        return rcopy(ref, ref, self.ss.at[i], self.rs.at[i], dev)

    def send(self, i, off, half, dev):
        c = self.cp(i, lax.rem(self.pc.t + off, 8), half, dev)
        c.start()
        self.sent.append(c)

    def recv(self, i, off, half):
        self.cp(i, lax.rem(self.pc.t + off, 8), half, self.pc.S).wait_recv()

    def recv_sib(self, i, off, half):
        self.cp(i, lax.rem(self.pc.sib_t + off, 8), half, self.pc.S).wait_recv()

    def start(self):
        pc = self.pc
        self.send(0, 0, 0, pc.XP)
        self.send(3, 0, 1, pc.XM)
        self.send(1, 0, 1, pc.XP)
        self.send(2, 0, 0, pc.XM)
        self.send(4, 0, 0, pc.S)
        self.send(5, 0, 1, pc.S)

    def first(self):
        pc = self.pc
        self.recv(0, 6, 0)
        self.send(6, 6, 0, pc.XP)
        self.recv(3, 2, 1)
        self.send(7, 2, 1, pc.XM)
        self.send(8, 6, 0, pc.S)
        self.send(11, 2, 1, pc.S)
        self.recv(1, 6, 1)
        self.send(9, 6, 1, pc.S)
        self.recv(2, 2, 0)
        self.send(10, 2, 0, pc.S)

    def second(self):
        pc = self.pc
        self.recv(6, 4, 0)
        self.send(12, 4, 0, pc.S)
        self.recv(7, 4, 1)
        self.send(13, 4, 1, pc.S)

    def finish(self):
        for i, off, half in (
            (4, 0, 0), (5, 0, 1), (8, 6, 0), (9, 6, 1), (10, 2, 0), (11, 2, 1), (12, 4, 0), (13, 4, 1),
        ):
            self.recv_sib(i, off, half)

    def end(self):
        for c in self.sent:
            c.wait_send()


def project_kernel(
    tok, wq, wk, wv, dout,
    X, W, Q, DO, KV,
    stage, kept, part_s, part_r,
    sw_s, sw_r, do_s, do_r, z_s, z_r, w_s, w_r, k_s, k_r, p_s, p_r,
):
    pc = Place()
    v, t, z, y = pc.v, pc.t, pc.z, pc.y
    pc.greet()
    swaps = []
    for k, (dev, vv) in enumerate(((pc.V, 1 - v), (pc.Y, v), (pc.D, 1 - v))):
        c = rcopy(tok.at[:, lanes(vv * HALF, HALF)], stage.at[v, y], sw_s.at[k], sw_r.at[k], dev)
        c.start()
        swaps.append(c)
    W[0, t] = wq[...]
    W[1, t] = wk[...]
    W[2, t] = wv[...]

    def w_at(tt, half):
        return W.at[:, tt, pl.ds(half * 160, 160)]

    wring = RingGather(pc, w_at, w_s, w_r)
    wring.start()
    stage[v, y] = tok[:, lanes(v * HALF, HALF)]
    do_copy = rcopy(
        dout.at[:, :, lanes((1 - v) * 128, 128)], DO.at[pl.ds(2 * v, 2)], do_s, do_r, pc.V
    )
    do_copy.start()
    DO[pl.ds(2 * v, 2)] = dout[:, :, lanes(v * 128, 128)]

    y2 = 1 - y
    for k, (a, b) in enumerate(((1 - v, y), (v, y2), (1 - v, y2))):
        rcopy(stage.at[a, b], stage.at[a, b], sw_s.at[k], sw_r.at[k], pc.V).wait_recv()
    for vv in range(2):
        low = stage[vv, 0].astype(F32)
        high = stage[vv, 1].astype(F32)
        for c in range(2):
            both = jnp.concatenate((low[8 * c : 8 * c + 8], high[8 * c : 8 * c + 8]), axis=0)
            X[2 * vv + c, z] = both.astype(BF16)

    z_sent = []

    def steps(d, cam):
        return 4 if (d == 0) == (cam < 2) else 3

    def z_ref(d, s, cam):
        off = (8 - s) if d == 0 else s
        return X.at[cam, lax.rem(z + off, 8)]

    def z_send(d, s, cam):
        ref = z_ref(d, s - 1, cam)
        c = rcopy(ref, ref, z_s.at[d, s - 1, cam], z_r.at[d, s - 1, cam], pc.ZP if d == 0 else pc.ZM)
        c.start()
        z_sent.append(c)

    def z_open(pair):
        for cam in (2 * pair, 2 * pair + 1):
            for d in range(2):
                z_send(d, 1, cam)

    def z_step(pair, s):
        for cam in (2 * pair, 2 * pair + 1):
            for d in range(2):
                if s <= steps(d, cam):
                    ref = z_ref(d, s, cam)
                    rcopy(ref, ref, z_s.at[d, s - 1, cam], z_r.at[d, s - 1, cam], pc.ZP).wait_recv()
                    if s < steps(d, cam):
                        z_send(d, s + 1, cam)

    p_sent = []

    def project(pair):
        rows = X[2 * pair : 2 * pair + 2].reshape(256, HALF)

        def one(m, carry):
            acc = jnp.dot(rows, W[m].reshape(HALF, 256), preferred_element_type=F32)
            left, right = acc[:, :128], acc[:, 128:]
            part_s[pair, m] = jnp.where(v == 0, right, left).astype(BF16)
            kept[pair, m] = jnp.where(v == 0, left, right)
            return carry

        lax.fori_loop(0, 3, one, 0)
        c = rcopy(part_s.at[pair], part_r.at[pair], p_s.at[pair], p_r.at[pair], pc.V)
        c.start()
        p_sent.append(c)

    def merge(pair):
        rcopy(part_s.at[pair], part_r.at[pair], p_s.at[pair], p_r.at[pair], pc.V).wait_recv()
        cams = slice(2 * pair, 2 * pair + 2)
        for m in range(3):
            whole = (kept[pair, m] + part_r[pair, m].astype(F32)).astype(BF16).reshape(2, 128, 128)
            if m == 0:
                Q[cams] = whole
            else:
                KV[m - 1, cams, t] = whole

    def kv_at(pair):
        return lambda tt, half: KV.at[half, pl.ds(2 * pair, 2), tt]

    kvrings = [RingGather(pc, kv_at(p), k_s.at[p], k_r.at[p]) for p in range(2)]

    z_open(0)
    z_step(0, 1)
    z_step(0, 2)
    z_step(0, 3)
    z_open(1)
    wring.first()
    z_step(0, 4)
    z_step(1, 1)
    wring.second()
    z_step(1, 2)
    wring.finish()
    project(0)
    z_step(1, 3)
    merge(0)
    kvrings[0].start()
    z_step(1, 4)
    project(1)
    kvrings[0].first()
    merge(1)
    kvrings[1].start()
    kvrings[0].second()
    kvrings[1].first()
    kvrings[1].second()
    kvrings[0].finish()
    kvrings[1].finish()
    do_copy.wait_recv()
    for ring in (wring, *kvrings):
        ring.end()
    for c in (*swaps, do_copy, *z_sent, *p_sent):
        c.wait_send()


def attend_kernel(pairs, masks, q_in, g_in, kv, att, dq, dkv, kc, vc, s_buf, dkc, dvc, bias, blk):
    for j in range(4):
        for i in range(4):
            hit = jnp.int32(0)
            for r in range(5):
                a, b = pairs[r, 0], pairs[r, 1]
                one = jnp.logical_or(
                    jnp.logical_and(a == i, b == j), jnp.logical_and(a == j, b == i)
                )
                hit = hit + one.astype(jnp.int32)
            level = jnp.where(hit > 0, 0.0, CLOSED).astype(F32)
            bias[pl.ds(j, 1), pl.ds(128 * i, 128)] = jnp.full((1, 128), level, F32)
    bias[pl.ds(4, 1), :] = jnp.full((1, ROWS), CLOSED, F32)

    def block64(n):
        return pl.ds(pl.multiple_of(n * 64, 64), 64)

    def squeeze(b, n):
        j, s = b // 16, lax.rem(b, 16)
        is_open = masks[j, s] > 0

        @pl.when(is_open)
        def _():
            kc[block64(n)] = kv[0, j, s // 2, block64(lax.rem(s, 2))]
            vc[block64(n)] = kv[1, j, s // 2, block64(lax.rem(s, 2))]
            blk[n] = j

        return n + is_open.astype(jnp.int32)

    count = lax.fori_loop(0, 64, squeeze, jnp.int32(0))
    chunks = (count + 3) // 4
    for e in range(3):

        @pl.when(count + e < 4 * chunks)
        def _():
            kc[block64(count + e)] = jnp.zeros((64, 128), BF16)
            vc[block64(count + e)] = jnp.zeros((64, 128), BF16)
            blk[count + e] = 4

    q = q_in[...].reshape(ROWS, 128)
    g = g_in[...].reshape(ROWS, 128)

    def chunk(c):
        return pl.ds(pl.multiple_of(c * 256, 256), 256)

    def nt(a, b):
        return lax.dot_general(a, b, (((1,), (1,)), ((), ())), preferred_element_type=F32)

    def tn(a, b):
        return lax.dot_general(a, b, (((0,), (0,)), ((), ())), preferred_element_type=F32)

    def score(c, top):
        s = nt(kc[chunk(c)], q) * SCALE
        parts = [s[64 * e : 64 * e + 64] + bias[pl.ds(blk[4 * c + e], 1), :] for e in range(4)]
        s = jnp.concatenate(parts, axis=0)
        s_buf[chunk(c)] = s
        return jnp.maximum(top, jnp.max(s, axis=0, keepdims=True))

    top = lax.fori_loop(0, chunks, score, jnp.full((1, ROWS), CLOSED, F32))

    def expo(c, total):
        e = jnp.exp(s_buf[chunk(c)] - top)
        s_buf[chunk(c)] = e
        return total + jnp.sum(e, axis=0, keepdims=True)

    total = lax.fori_loop(0, chunks, expo, jnp.zeros((1, ROWS), F32))
    inv = 1.0 / total

    def mix(c, acc):
        p = (s_buf[chunk(c)] * inv).astype(BF16)
        return acc + tn(vc[chunk(c)], p)

    mixed = lax.fori_loop(0, chunks, mix, jnp.zeros((128, ROWS), F32))
    out = jnp.transpose(mixed).astype(BF16)
    att[...] = out.reshape(4, 128, 128)
    prod = out.astype(F32) * g.astype(F32)
    delta = jnp.sum(jnp.transpose(prod), axis=0, keepdims=True)

    def back(c, acc):
        w = s_buf[chunk(c)] * inv
        dp = nt(vc[chunk(c)], g)
        ds = (w * (dp - delta) * SCALE).astype(BF16)
        dkc[chunk(c)] = jnp.dot(ds, q, preferred_element_type=F32).astype(BF16)
        dvc[chunk(c)] = jnp.dot(w.astype(BF16), g, preferred_element_type=F32).astype(BF16)
        return acc + tn(kc[chunk(c)], ds)

    dq_t = lax.fori_loop(0, chunks, back, jnp.zeros((128, ROWS), F32))
    dq[...] = jnp.transpose(dq_t).astype(BF16).reshape(4, 128, 128)

    def spread(b, n):
        j, s = b // 16, lax.rem(b, 16)
        is_open = masks[j, s] > 0

        @pl.when(is_open)
        def _():
            dkv[0, j, s // 2, block64(lax.rem(s, 2))] = dkc[block64(n)]
            dkv[1, j, s // 2, block64(lax.rem(s, 2))] = dvc[block64(n)]

        @pl.when(jnp.logical_not(is_open))
        def _():
            dkv[0, j, s // 2, block64(lax.rem(s, 2))] = jnp.zeros((64, 128), BF16)
            dkv[1, j, s // 2, block64(lax.rem(s, 2))] = jnp.zeros((64, 128), BF16)

        return n + is_open.astype(jnp.int32)

    lax.fori_loop(0, 64, spread, jnp.int32(0))


class RingScatter:
    def __init__(self, pc, own, sib_src, sib_r, bufs, bufr, ss, rs):
        self.pc, self.own, self.sib_src, self.sib_r = pc, own, sib_src, sib_r
        self.bufs, self.bufr, self.ss, self.rs = bufs, bufr, ss, rs
        self.sent = []

    def sib_cp(self, k):
        return rcopy(self.sib_src(k), self.sib_r.at[k], self.ss.at[6 + k], self.rs.at[6 + k], self.pc.S)

    def sib_send(self, k):
        c = self.sib_cp(k)
        c.start()
        self.sent.append(c)

    def sib_wait(self, k):
        self.sib_cp(k).wait_recv()

    def cp(self, i, dev):
        return rcopy(self.bufs.at[i], self.bufr.at[i], self.ss.at[i], self.rs.at[i], dev)

    def term(self, k, half):
        return self.own(k, half) + self.sib_r[k, half].astype(F32)

    def push(self, i, value, dev):
        self.bufs[i] = value.astype(BF16)
        c = self.cp(i, dev)
        c.start()
        self.sent.append(c)

    def wait(self, i):
        self.cp(i, self.pc.S).wait_recv()
        return self.bufr[i].astype(F32)

    def far(self):
        self.sib_wait(0)
        self.push(0, self.term(0, 0), self.pc.XP)
        self.push(1, self.term(0, 1), self.pc.XM)

    def near(self):
        self.sib_wait(1)
        self.push(3, self.term(1, 1), self.pc.XP)
        self.sib_wait(2)
        self.push(4, self.term(2, 0), self.pc.XM)

    def near2(self):
        self.push(2, self.term(1, 0) + self.wait(0), self.pc.XP)
        self.push(5, self.term(2, 1) + self.wait(1), self.pc.XM)

    def last(self, half):
        if half == 0:
            self.sib_wait(3)
        return self.term(3, half) + self.wait(2 + half) + self.wait(4 + half)

    def end(self):
        for c in self.sent:
            c.wait_send()


def grads_kernel(
    X, W, att, dq, dkv,
    att_out, tgrad, gq, gk, gv,
    G, TG, zbs, zbr, fin, ys, yr, sib1, b1s, b1r, wt, sib2s, sib2r, b2s, b2r,
    a_s, a_r, e_s, e_r, z_s, z_r, y_s, y_r, d_s, d_r, w_s, w_r,
):
    pc = Place()
    v, z, y, x, core = pc.v, pc.z, pc.y, pc.x, pc.core
    pc.greet()
    sent = []

    def go(c):
        c.start()
        sent.append(c)

    def shifted(k):
        return lax.rem(x + (2, 1, 3, 0)[k], 4)

    dring = RingScatter(
        pc,
        lambda k, half: dkv[half, :, 2 * shifted(k) + core].astype(F32),
        lambda k: dkv.at[:, :, 2 * shifted(k) + 1 - core],
        sib1, b1s, b1r, d_s, d_r,
    )
    for k in range(4):
        dring.sib_send(k)
    own_cols = lanes(v * 128, 128)
    go(rcopy(att.at[pl.ds(2 - 2 * v, 2)], att_out.at[:, :, own_cols], a_s, a_r, pc.V))

    def g_cols(m, head):
        return lanes(m * 256 + head * 128, 128)

    def g_copy(m, head):
        ref = G.at[:, g_cols(m, head)]
        return rcopy(ref, ref, e_s.at[m], e_r.at[m], pc.V)

    dring.far()
    G[:, g_cols(0, v)] = dq[...].reshape(ROWS, 128)
    go(g_copy(0, v))
    att_out[:, :, own_cols] = att[pl.ds(2 * v, 2)]
    dring.near()
    dring.near2()
    for half in range(2):
        G[:, g_cols(1 + half, v)] = dring.last(half).astype(BF16).reshape(ROWS, 128)
        go(g_copy(1 + half, v))
    for m in range(3):
        g_copy(m, 1 - v).wait_recv()

    def token_term(pair):
        rows = G[256 * pair : 256 * pair + 256, :]

        def some(i, carry):
            acc = jnp.zeros((256, 640), F32)
            for m in range(3):
                weight = W[m, pl.ds(2 * i, 2)].reshape(640, 256)
                acc = acc + lax.dot_general(
                    rows[:, 256 * m : 256 * m + 256], weight, (((1,), (1,)), ((), ())),
                    preferred_element_type=F32,
                )
            TG[2 * pair : 2 * pair + 2, :, :, lanes(i * 640, 640)] = acc.reshape(2, 8, 16, 640)
            return carry

        lax.fori_loop(0, 4, some, 0)

    def steps(d, cam):
        return 4 if (d == 0) == (cam < 2) else 3

    def z_cp(d, s, cam):
        return rcopy(
            zbs.at[d, s - 1, cam], zbr.at[d, s - 1, cam], z_s.at[d, s - 1, cam], z_r.at[d, s - 1, cam],
            pc.ZP if d == 0 else pc.ZM,
        )

    def z_step(pair, s):
        for cam in (2 * pair, 2 * pair + 1):
            for d in range(2):
                n = steps(d, cam)
                if s <= n:
                    far = n - s + 1
                    value = TG[cam, lax.rem(z + (far if d == 0 else 8 - far), 8)]
                    if s > 1:
                        z_cp(d, s - 1, cam).wait_recv()
                        value = value + zbr[d, s - 2, cam].astype(F32)
                    zbs[d, s - 1, cam] = value.astype(BF16)
                    go(z_cp(d, s, cam))

    def z_last(pair):
        for cam in (2 * pair, 2 * pair + 1):
            value = TG[cam, z]
            for d in range(2):
                n = steps(d, cam)
                z_cp(d, n, cam).wait_recv()
                value = value + zbr[d, n - 1, cam].astype(F32)
            fin[cam] = value

    def w_own(k, half):
        return wt[k, :, pl.ds(half * 160, 160)]

    wring = RingScatter(pc, w_own, lambda k: sib2s.at[k], sib2r, b2s, b2r, w_s, w_r)

    def weight_term(k):
        cols = X[:, :, :, lanes(shifted(k) * 640, 640)].reshape(ROWS, 640)
        for m in range(3):
            acc = lax.dot_general(
                cols, G[:, 256 * m : 256 * m + 256], (((0,), (0,)), ((), ())),
                preferred_element_type=F32,
            )
            low, high = acc[:320], acc[320:]
            wt[k, m] = jnp.where(core == 0, low, high)
            other = jnp.where(core == 0, high, low).astype(BF16)
            sib2s[k, 0, m] = other[:160]
            sib2s[k, 1, m] = other[160:]
        wring.sib_send(k)

    token_term(0)
    z_step(0, 1)
    token_term(1)
    z_step(1, 1)
    weight_term(0)
    weight_term(1)
    wring.far()
    z_step(0, 2)
    z_step(1, 2)
    weight_term(2)
    wring.near()
    z_step(0, 3)
    z_step(1, 3)
    weight_term(3)
    wring.near2()
    z_step(0, 4)
    z_step(1, 4)
    z_last(0)
    z_last(1)

    def piece(vv, yy):
        rows = pl.ds(pl.multiple_of(8 * yy, 8), 8)
        return jnp.concatenate((fin[2 * vv, rows], fin[2 * vv + 1, rows]), axis=0)

    def y_cp(k):
        return rcopy(ys.at[k], yr.at[k], y_s.at[k], y_r.at[k], (pc.V, pc.Y, pc.D)[k])

    for k, (vv, yy) in enumerate(((1 - v, y), (v, 1 - y), (1 - v, 1 - y))):
        ys[k] = piece(vv, yy).astype(BF16)
        go(y_cp(k))
    for half in range(2):
        value = wring.last(half)
        rows = slice(160 * half, 160 * half + 160)
        for m, out in enumerate((gq, gk, gv)):
            out[rows] = value[m].astype(BF16)
    for k in range(3):
        y_cp(k).wait_recv()
    tgrad[:, lanes(v * HALF, HALF)] = (piece(v, y) + yr[1].astype(F32)).astype(BF16)
    tgrad[:, lanes((1 - v) * HALF, HALF)] = (yr[0].astype(F32) + yr[2].astype(F32)).astype(BF16)
    rcopy(att.at[pl.ds(2 - 2 * v, 2)], att_out.at[:, :, lanes((1 - v) * 128, 128)], a_s, a_r, pc.V).wait_recv()
    for ring in (dring, wring):
        ring.end()
    for c in sent:
        c.wait_send()


def on_device(tokens, query_weight, key_weight, value_weight, out_grad, pairs, block_masks):
    vm = pl.BlockSpec(memory_space=pltpu.VMEM)
    sm = pl.BlockSpec(memory_space=pltpu.SMEM)
    dma = pltpu.SemaphoreType.DMA

    def shape(*dims):
        return jax.ShapeDtypeStruct(dims, BF16)

    X, W, Q, DO, KV = pl.pallas_call(
        project_kernel,
        out_shape=(
            shape(4, 8, 16, HALF), shape(3, 8, 320, 256), shape(4, 128, 128), shape(4, 128, 128),
            shape(2, 4, 8, 128, 128),
        ),
        in_specs=[vm] * 5,
        out_specs=[vm] * 5,
        scratch_shapes=[
            pltpu.VMEM((2, 2, 16, HALF), BF16),
            pltpu.VMEM((2, 3, 256, 128), F32),
            pltpu.VMEM((2, 3, 256, 128), BF16),
            pltpu.VMEM((2, 3, 256, 128), BF16),
            dma((3,)), dma((3,)), dma, dma,
            dma((2, 4, 4)), dma((2, 4, 4)),
            dma((14,)), dma((14,)), dma((2, 14)), dma((2, 14)), dma((2,)), dma((2,)),
        ],
        compiler_params=pltpu.CompilerParams(
            collective_id=0, has_side_effects=True, vmem_limit_bytes=VMEM_LIMIT
        ),
        name="project",
    )(tokens.reshape(16, 2 * HALF), query_weight, key_weight, value_weight, out_grad)

    att, dq, dkv = pl.pallas_call(
        attend_kernel,
        out_shape=(shape(4, 128, 128), shape(4, 128, 128), shape(2, 4, 8, 128, 128)),
        in_specs=[sm, sm, vm, vm, vm],
        out_specs=[vm] * 3,
        scratch_shapes=[
            pltpu.VMEM((4096, 128), BF16),
            pltpu.VMEM((4096, 128), BF16),
            pltpu.VMEM((4096, ROWS), F32),
            pltpu.VMEM((4096, 128), BF16),
            pltpu.VMEM((4096, 128), BF16),
            pltpu.VMEM((8, ROWS), F32),
            pltpu.SMEM((64,), jnp.int32),
        ],
        compiler_params=pltpu.CompilerParams(vmem_limit_bytes=VMEM_LIMIT),
        name="attend",
    )(pairs, block_masks, Q, DO, KV)

    att_out, tgrad, gq, gk, gv = pl.pallas_call(
        grads_kernel,
        out_shape=(
            shape(2, 128, 256), shape(16, 2 * HALF), shape(320, 256), shape(320, 256), shape(320, 256),
        ),
        in_specs=[vm] * 5,
        out_specs=[vm] * 5,
        scratch_shapes=[
            pltpu.VMEM((ROWS, 768), BF16),
            pltpu.VMEM((4, 8, 16, HALF), F32),
            pltpu.VMEM((2, 4, 4, 16, HALF), BF16),
            pltpu.VMEM((2, 4, 4, 16, HALF), BF16),
            pltpu.VMEM((4, 16, HALF), F32),
            pltpu.VMEM((3, 16, HALF), BF16),
            pltpu.VMEM((3, 16, HALF), BF16),
            pltpu.VMEM((4, 2, 4, 128, 128), BF16),
            pltpu.VMEM((6, 4, 128, 128), BF16),
            pltpu.VMEM((6, 4, 128, 128), BF16),
            pltpu.VMEM((4, 3, 320, 256), F32),
            pltpu.VMEM((4, 2, 3, 160, 256), BF16),
            pltpu.VMEM((4, 2, 3, 160, 256), BF16),
            pltpu.VMEM((6, 3, 160, 256), BF16),
            pltpu.VMEM((6, 3, 160, 256), BF16),
            dma, dma, dma((3,)), dma((3,)),
            dma((2, 4, 4)), dma((2, 4, 4)), dma((3,)), dma((3,)),
            dma((10,)), dma((10,)), dma((10,)), dma((10,)),
        ],
        compiler_params=pltpu.CompilerParams(
            collective_id=1, has_side_effects=True, vmem_limit_bytes=VMEM_LIMIT
        ),
        name="grads",
    )(X, W, att, dq, dkv)
    return (att_out, tgrad.reshape(2, 8, 2 * HALF), gq, gk, gv)


def solution(mesh):
    return jax.shard_map(
        on_device,
        mesh=mesh,
        in_specs=(
            P("view", ("tm", "head"), None),
            P(("view", "tm"), "head"),
            P(("view", "tm"), "head"),
            P(("view", "tm"), "head"),
            P("view", "tm", "head"),
            P(),
            P(),
        ),
        out_specs=(
            P("view", "tm", "head"),
            P("view", ("tm", "head"), None),
            P(("view", "tm"), "head"),
            P(("view", "tm"), "head"),
            P(("view", "tm"), "head"),
        ),
        check_vma=False,
    )
```

time: 750 us -> 158 us (0.21)
  waiting for transfers between devices: 587 us -> 0 us
  Pallas kernels: 0 us -> 147 us
  matrix products: 88.6 us -> 0 us
  local copies, waits for them, and re-layouts: 47 us -> 9.29 us
  between operations: 14.1 us -> 0.65 us
    unnamed x11 -> x0, waiting for transfers between devices: 269 us -> none
    all_gather x6 -> x0, waiting for transfers between devices: 257 us -> none  [the longest x1 92.1 us: on_device(): full = lax.all_gather(tokens, 'head', axis=1, tiled=True)]
    pallas_call x0 -> x3, Pallas kernels: none -> 147 us  [the longest x1 68.1 us: on_device(): pl.pallas_call(project_kernel, out_shape=(shape(4, 8, 16, HALF), shape(3,...]
    dot_general x63 -> x0, matrix products: 88.6 us -> none  [the longest x8 18.4 us: mix_values(): jnp.einsum('ctak,kae->ctae', probs, block_values, preferred_element_type=...]
    reduce_scatter x1 -> x0, waiting for transfers between devices: 60.3 us -> none  [on_device(): lax.psum_scatter(key_terms.reshape(n_shards * rows, 2 * width).astype(jnp...]
    unnamed x32 -> x6, local copies, waits for them, and re-layouts: 24.8 us -> 9.29 us
    dynamic_update_slice x16 -> x0, local copies, waits for them, and re-layouts: 8.43 us -> none  [on_device(): lax.scan(back_step, head_zeros, (key_blocks, value_blocks, allowed_blocks))]
  transfers between devices with their start and end apart: 9 -> 0, of which waited for: 9 -> 0; matrix products, arithmetic and copies ran while one was open for 7% -> 0% of each run, Pallas kernels for 0% -> 0%
where the time goes in v1:
time: 158 us; the launch traced here: 156 us
  Pallas kernels  147 us (93%)
  local copies, waits for them, and re-layouts  9.29 us (6%)
    pallas_call x1, Pallas kernels, on_device(): pl.pallas_call(project_kernel, out_shape=(shape(4, 8, 16, HALF), shape(3,...  68.1 us
    pallas_call x1, Pallas kernels, on_device(): pl.pallas_call(grads_kernel, out_shape=(shape(2, 128, 256), shape(16, 2 *...  61.3 us
    pallas_call x1, Pallas kernels, on_device(): pl.pallas_call(attend_kernel, out_shape=(shape(4, 128, 128), shape(4, 128...  17.2 us
    unnamed x6, local copies, waits for them, and re-layouts  9.29 us

profile of v1, /device:TPU:2, one launch (start us, length us, event | category | flops | bytes accessed | tf_op | source)
XLA Modules:
  0.0 156.4 jit_solution(13863156479837380019)
XLA Ops:
  0.6 1.4 copy.12.pairs
  2.0 68.1 %project.1 = (bf16[4,8,16,2560]{3,2,1,0:T(8,128)(2,1)}, bf16[3,8,320,256]{3,2,1,0:T(8,128)(2,1)}, bf16[4,128,128]{2,1,0:T(8,128)(2,1)}, bf16[4,128,128]{2,1,0:T(8,128)(2,1)}, bf16[2,4,8,128,128]{4,3,2,1,0:T(8,128)(2,1)}) custom-call(bf16[16,5120]{1,0:T(8,128)(2,1)} %bitcast.3, bf16[320,256]{1,0:T(8,128)(2,1)} %wq.1, bf16[320,256]{1,0:T(8,128)(2,1)} %wk.1, ...), custom_call_target="tpu_custom_call" | custom-call | tf_op jit(solution)/shard_map/project/pallas_call | solution.py:585
  70.1 17.2 %attend.1 = (bf16[4,128,128]{2,1,0:T(8,128)(2,1)}, bf16[4,128,128]{2,1,0:T(8,128)(2,1)}, bf16[2,4,8,128,128]{4,3,2,1,0:T(8,128)(2,1)}) custom-call(s32[5,2]{1,0:T(8,128)} %copy.12.pairs, s32[4,16]{1,0:T(4,128)} %masks.1, bf16[4,128,128]{2,1,0:T(8,128)(2,1)} %get-tuple-element.20.q_in, bf16[4,128,128]{2,1,0:T(8,128)(2,1)} %get-tuple-element.21.g_in, ...), custom_call_target="tpu_custom_call" | custom-call | tf_op jit(solution)/shard_map/attend/pallas_call | solution.py:608
  87.2 61.3 %grads.1 = (bf16[2,128,256]{2,1,0:T(8,128)(2,1)}, bf16[16,5120]{1,0:T(8,128)(2,1)}, bf16[320,256]{1,0:T(8,128)(2,1)}, bf16[320,256]{1,0:T(8,128)(2,1)}, bf16[320,256]{1,0:T(8,128)(2,1)}) custom-call(bf16[4,8,16,2560]{3,2,1,0:T(8,128)(2,1)} %get-tuple-element.18.X, bf16[3,8,320,256]{3,2,1,0:T(8,128)(2,1)} %get-tuple-element.19.W, ...), custom_call_target="tpu_custom_call" | custom-call | tf_op jit(solution)/shard_map/grads/pallas_call | solution.py:626
  148.5 1.6 %copy.18 = bf16[2,128,256]{2,1,0:T(8,128)(2,1)} copy(bf16[2,128,256]{2,1,0:T(8,128)(2,1)} %get-tuple-element.36) | data formatting | bytes 262144
  150.1 1.6 %copy.19 = bf16[2,8,5120]{2,1,0:T(8,128)(2,1)} copy(bf16[2,8,5120]{2,1,0:T(8,128)(2,1)} %bitcast.2) | data formatting | bytes 327680
  151.7 1.6 %copy.20 = bf16[320,256]{1,0:T(8,128)(2,1)} copy(bf16[320,256]{1,0:T(8,128)(2,1)} %get-tuple-element.38) | data formatting | bytes 327680
  153.3 1.6 %copy.21 = bf16[320,256]{1,0:T(8,128)(2,1)} copy(bf16[320,256]{1,0:T(8,128)(2,1)} %get-tuple-element.39) | data formatting | bytes 327680
  154.8 1.6 %copy.22 = bf16[320,256]{1,0:T(8,128)(2,1)} copy(bf16[320,256]{1,0:T(8,128)(2,1)} %get-tuple-element.40) | data formatting | bytes 327680

commit v2 on v1

v2 whole, which is shorter than its diff:
```python
import math

import jax
import jax.numpy as jnp
from jax import lax
from jax.experimental import pallas as pl
from jax.experimental.pallas import tpu as pltpu
from jax.sharding import PartitionSpec as P

MESH = pl.DeviceIdType.MESH
F32 = jnp.float32
BF16 = jnp.bfloat16
VMEM_LIMIT = 58 * 1024 * 1024

HALF = 2560
ROWS = 512
SCALE = 1.0 / math.sqrt(128)
CLOSED = -1e30
Z_STEPS = ((4, 3), (3, 4), (4, 3))
LOG2E = math.log2(math.e)


class Place:
    def __init__(self):
        self.v = lax.axis_index("view")
        self.t = lax.axis_index("tm")
        self.h = lax.axis_index("head")
        v, t, h = self.v, self.t, self.h
        self.x, self.core = t // 2, lax.rem(t, 2)
        self.z, self.y = h // 2, lax.rem(h, 2)
        self.sib_t = t + 1 - 2 * self.core
        other_h = h + 1 - 2 * self.y
        self.V = {"view": 1 - v}
        self.Y = {"head": other_h}
        self.D = {"view": 1 - v, "head": other_h}
        self.ZP = {"head": lax.rem(h + 2, 16)}
        self.ZM = {"head": lax.rem(h + 14, 16)}
        self.XP = {"tm": lax.rem(t + 2, 8)}
        self.XM = {"tm": lax.rem(t + 6, 8)}
        self.S = {"tm": self.sib_t}

    def greet(self):
        bar = pltpu.get_barrier_semaphore()
        peers = (self.V, self.Y, self.D, self.ZP, self.ZM, self.XP, self.XM, self.S)
        for peer in peers:
            pl.semaphore_signal(bar, inc=1, device_id=peer, device_id_type=MESH)
        pl.semaphore_wait(bar, len(peers))


def rcopy(src, dst, ss, rs, dev):
    return pltpu.make_async_remote_copy(
        src_ref=src, dst_ref=dst, send_sem=ss, recv_sem=rs, device_id=dev, device_id_type=MESH
    )


def lanes(start, size):
    return pl.ds(pl.multiple_of(start, 128), size)


class RingGather:
    def __init__(self, pc, at, ss, rs):
        self.pc, self.at, self.ss, self.rs = pc, at, ss, rs
        self.sent = []

    def cp(self, i, t, half, dev):
        ref = self.at(t, half)
        return rcopy(ref, ref, self.ss.at[i], self.rs.at[i], dev)

    def send(self, i, off, half, dev):
        c = self.cp(i, lax.rem(self.pc.t + off, 8), half, dev)
        c.start()
        self.sent.append(c)

    def recv(self, i, off, half):
        self.cp(i, lax.rem(self.pc.t + off, 8), half, self.pc.S).wait_recv()

    def recv_sib(self, i, off, half):
        self.cp(i, lax.rem(self.pc.sib_t + off, 8), half, self.pc.S).wait_recv()

    def start(self):
        pc = self.pc
        self.send(0, 0, 0, pc.XP)
        self.send(3, 0, 1, pc.XM)
        self.send(1, 0, 1, pc.XP)
        self.send(2, 0, 0, pc.XM)
        self.send(4, 0, 0, pc.S)
        self.send(5, 0, 1, pc.S)

    def first(self):
        pc = self.pc
        self.recv(0, 6, 0)
        self.send(6, 6, 0, pc.XP)
        self.recv(3, 2, 1)
        self.send(7, 2, 1, pc.XM)
        self.send(8, 6, 0, pc.S)
        self.send(11, 2, 1, pc.S)
        self.recv(1, 6, 1)
        self.send(9, 6, 1, pc.S)
        self.recv(2, 2, 0)
        self.send(10, 2, 0, pc.S)

    def second(self):
        pc = self.pc
        self.recv(6, 4, 0)
        self.send(12, 4, 0, pc.S)
        self.recv(7, 4, 1)
        self.send(13, 4, 1, pc.S)

    def finish(self):
        for i, off, half in (
            (4, 0, 0), (5, 0, 1), (8, 6, 0), (9, 6, 1), (10, 2, 0), (11, 2, 1), (12, 4, 0), (13, 4, 1),
        ):
            self.recv_sib(i, off, half)

    def end(self):
        for c in self.sent:
            c.wait_send()


class RingScatter:
    def __init__(self, pc, own, sib_src, sib_r, bufs, bufr, ss, rs):
        self.pc, self.own, self.sib_src, self.sib_r = pc, own, sib_src, sib_r
        self.bufs, self.bufr, self.ss, self.rs = bufs, bufr, ss, rs
        self.sent = []

    def sib_cp(self, k):
        return rcopy(self.sib_src(k), self.sib_r.at[k], self.ss.at[6 + k], self.rs.at[6 + k], self.pc.S)

    def sib_send(self, k):
        c = self.sib_cp(k)
        c.start()
        self.sent.append(c)

    def sib_wait(self, k):
        self.sib_cp(k).wait_recv()

    def cp(self, i, dev):
        return rcopy(self.bufs.at[i], self.bufr.at[i], self.ss.at[i], self.rs.at[i], dev)

    def term(self, k, half):
        return self.own(k, half) + self.sib_r[k, half].astype(F32)

    def push(self, i, value, dev):
        self.bufs[i] = value.astype(BF16)
        c = self.cp(i, dev)
        c.start()
        self.sent.append(c)

    def wait(self, i):
        self.cp(i, self.pc.S).wait_recv()
        return self.bufr[i].astype(F32)

    def far(self):
        self.sib_wait(0)
        self.push(0, self.term(0, 0), self.pc.XP)
        self.push(1, self.term(0, 1), self.pc.XM)

    def near(self):
        self.sib_wait(1)
        self.push(3, self.term(1, 1), self.pc.XP)
        self.sib_wait(2)
        self.push(4, self.term(2, 0), self.pc.XM)

    def near2(self):
        self.push(2, self.term(1, 0) + self.wait(0), self.pc.XP)
        self.push(5, self.term(2, 1) + self.wait(1), self.pc.XM)

    def last(self, half):
        if half == 0:
            self.sib_wait(3)
        return self.term(3, half) + self.wait(2 + half) + self.wait(4 + half)

    def end(self):
        for c in self.sent:
            c.wait_send()


def fused_kernel(
    tok, wq, wk, wv, dout, pairs, masks,
    att_out, tgrad, gq, gk, gv,
    X, W, Q, DO, KV, stage, kept, part_s, part_r, relay,
    link, bias, s_buf, ds_buf, tops, stat, acc, att, dkv,
    G, TG, zbs, zbr, fin, ys, yr, sib1, b1s, b1r, wt, sib2s, sib2r, b2s, b2r,
    sw_s, sw_r, do_s, do_r, z_s, z_r, w_s, w_r, k_s, k_r, p_s, p_r, r_s, r_r,
    a_s, a_r, e_s, e_r, t_s, t_r, y_s, y_r, d_s, d_r, f_s, f_r,
):
    pc = Place()
    v, t, z, y, x, core = pc.v, pc.t, pc.z, pc.y, pc.x, pc.core
    pc.greet()
    swaps = []
    for k, (dev, vv) in enumerate(((pc.V, 1 - v), (pc.Y, v), (pc.D, 1 - v))):
        c = rcopy(tok.at[:, lanes(vv * HALF, HALF)], stage.at[v, y], sw_s.at[k], sw_r.at[k], dev)
        c.start()
        swaps.append(c)
    W[0, t] = wq[...]
    W[1, t] = wk[...]
    W[2, t] = wv[...]

    def w_at(tt, half):
        return W.at[:, tt, pl.ds(half * 160, 160)]

    wring = RingGather(pc, w_at, w_s, w_r)
    wring.start()
    stage[v, y] = tok[:, lanes(v * HALF, HALF)]
    do_copy = rcopy(
        dout.at[:, :, lanes((1 - v) * 128, 128)], DO.at[pl.ds(2 * v, 2)], do_s, do_r, pc.V
    )
    do_copy.start()
    DO[pl.ds(2 * v, 2)] = dout[:, :, lanes(v * 128, 128)]

    def make_bias():
        for j in range(4):
            for i in range(4):
                hit = jnp.int32(0)
                for r in range(5):
                    a, b = pairs[0, r], pairs[1, r]
                    one = jnp.logical_or(
                        jnp.logical_and(a == i, b == j), jnp.logical_and(a == j, b == i)
                    )
                    hit = hit + one.astype(jnp.int32)
                level = jnp.where(hit > 0, 0.0, CLOSED).astype(F32)
                link[pl.ds(j, 1), pl.ds(128 * i, 128)] = jnp.full((1, 128), level, F32)
        for j in range(4):
            for s in range(16):
                level = jnp.where(masks[j, s] > 0, 0.0, CLOSED).astype(F32)
                bias[j, pl.ds(s, 1), :] = link[pl.ds(j, 1), :] + level

    make_bias()
    y2 = 1 - y
    for k, (a, b) in enumerate(((1 - v, y), (v, y2), (1 - v, y2))):
        rcopy(stage.at[a, b], stage.at[a, b], sw_s.at[k], sw_r.at[k], pc.V).wait_recv()
    for vv in range(2):
        low = stage[vv, 0].astype(F32)
        high = stage[vv, 1].astype(F32)
        for c in range(2):
            both = jnp.concatenate((low[8 * c : 8 * c + 8], high[8 * c : 8 * c + 8]), axis=0)
            X[2 * vv + c, z] = both.astype(BF16)

    sent = []
    cam_of = (y, 2, 3)

    def z_block(d, s):
        return lax.rem(z + ((8 - s) if d == 0 else s), 8)

    def z_cp(d, s, u):
        ref = X.at[cam_of[u], z_block(d, s - 1)]
        return rcopy(
            ref, ref, z_s.at[d, s - 1, u], z_r.at[d, s - 1, u], pc.ZP if d == 0 else pc.ZM
        )

    def z_send(d, s, u):
        c = z_cp(d, s, u)
        c.start()
        sent.append(c)

    def z_open(u):
        for d in range(2):
            z_send(d, 1, u)

    def z_step(u, s):
        for d in range(2):
            if s <= Z_STEPS[u][d]:
                ref = X.at[cam_of[u], z_block(d, s)]
                rcopy(ref, ref, z_s.at[d, s - 1, u], z_r.at[d, s - 1, u], pc.ZP).wait_recv()
                if s < Z_STEPS[u][d]:
                    z_send(d, s + 1, u)
                if u == 0:
                    c = rcopy(ref, relay.at[d, s - 1], r_s.at[0, d, s - 1], r_r.at[0, d, s - 1], pc.V)
                    c.start()
                    sent.append(c)

    def relay_on(s):
        for d in range(2):
            if s <= Z_STEPS[0][d]:
                ref = relay.at[d, s - 1]
                rcopy(ref, ref, r_s.at[0, d, s - 1], r_r.at[0, d, s - 1], pc.V).wait_recv()
                there = X.at[y, z_block(d, s)]
                c = rcopy(ref, there, r_s.at[1, d, s - 1], r_r.at[1, d, s - 1], pc.D)
                c.start()
                sent.append(c)

    def relay_end():
        for s in range(1, 5):
            for d in range(2):
                if s <= Z_STEPS[0][d]:
                    ref = X.at[1 - y, z_block(d, s)]
                    rcopy(ref, ref, r_s.at[1, d, s - 1], r_r.at[1, d, s - 1], pc.D).wait_recv()

    def go(c):
        c.start()
        sent.append(c)


    def project(pair):
        def one(m, carry):
            rows = X[2 * pair : 2 * pair + 2].reshape(256, HALF)
            acc = jnp.dot(rows, W[m].reshape(HALF, 256), preferred_element_type=F32)
            left, right = acc[:, :128], acc[:, 128:]
            part_s[pair, m] = jnp.where(v == 0, right, left).astype(BF16)
            kept[pair, m] = jnp.where(v == 0, left, right)
            return carry

        lax.fori_loop(1, 3, one, 0)
        go(p_cp(pair, 1))
        lax.fori_loop(0, 1, one, 0)
        go(p_cp(pair, 0))

    def p_cp(pair, i):
        part = pl.ds(0, 1) if i == 0 else pl.ds(1, 2)
        return rcopy(
            part_s.at[pair, part], part_r.at[pair, part], p_s.at[pair, i], p_r.at[pair, i], pc.V
        )

    def whole(pair, m):
        return (kept[pair, m] + part_r[pair, m].astype(F32)).astype(BF16).reshape(2, 128, 128)

    def merge(pair):
        p_cp(pair, 1).wait_recv()
        for m in (1, 2):
            KV[m - 1, 2 * pair : 2 * pair + 2, t] = whole(pair, m)

    def kv_at(pair):
        return lambda tt, half: KV.at[half, pl.ds(2 * pair, 2), tt]

    kvrings = [RingGather(pc, kv_at(p), k_s.at[p], k_r.at[p]) for p in range(2)]

    def nt(a, b):
        return lax.dot_general(a, b, (((1,), (1,)), ((), ())), preferred_element_type=F32)

    def tn(a, b):
        return lax.dot_general(a, b, (((0,), (0,)), ((), ())), preferred_element_type=F32)

    def keys(m, c):
        return KV[m, c // 2, pl.ds(4 * lax.rem(c, 2), 4)].reshape(512, 128)

    def chunk(c):
        return pl.ds(pl.multiple_of(c * 512, 512), 512)

    def forward(low, high, kp):
        qs = slice(256 * low, 256 * high)
        width = 256 * (high - low)

        def step(c, carry):
            top, total = carry
            s = nt(keys(0, c), Q[2 * low : 2 * high].reshape(width, 128)) * (SCALE * LOG2E)
            block = 8 * lax.rem(c, 2)
            parts = [
                s[64 * e : 64 * e + 64] + bias[c // 2, pl.ds(block + e, 1), qs] for e in range(8)
            ]
            s = jnp.concatenate(parts, axis=0)
            new_top = jnp.maximum(top, jnp.max(s, axis=0, keepdims=True))
            fade = jnp.exp2(top - new_top)
            e = jnp.exp2(s - new_top)
            s_buf[chunk(c), qs] = e
            tops[pl.ds(c, 1), qs] = new_top
            acc[:, qs] = acc[:, qs] * fade + tn(keys(1, c), e.astype(BF16))
            return new_top, total * fade + jnp.sum(e, axis=0, keepdims=True)

        if kp == 0:
            start = (jnp.full((1, width), CLOSED, F32), jnp.zeros((1, width), F32))
            acc[:, qs] = jnp.zeros((128, width), F32)
        else:
            start = (stat[0:1, qs], stat[1:2, qs])
        top, total = lax.fori_loop(4 * kp, 4 * kp + 4, step, start)
        stat[0:1, qs] = top
        stat[1:2, qs] = total

    def settle():
        inv = 1.0 / stat[1:2, :]
        out = jnp.transpose(acc[...] * inv).astype(BF16)
        att[...] = out.reshape(4, 128, 128)
        prod = out.astype(F32) * DO[...].reshape(ROWS, 128).astype(F32)
        acc[...] = jnp.zeros((128, ROWS), F32)
        return inv, jnp.sum(jnp.transpose(prod), axis=0, keepdims=True)

    def back(cam):
        def step(c, carry):
            w = s_buf[chunk(c), :] * (jnp.exp2(tops[pl.ds(c, 1), :] - stat[0:1, :]) * inv)
            g = DO[...].reshape(ROWS, 128)
            dv = jnp.dot(w.astype(BF16), g, preferred_element_type=F32)
            ds = (w * (nt(keys(1, c), g) - delta)).astype(BF16)
            ds_buf[chunk(c), :] = ds
            dk = jnp.dot(ds, Q[...].reshape(ROWS, 128), preferred_element_type=F32) * SCALE
            at = pl.ds(4 * lax.rem(c, 2), 4)
            dkv[0, cam, at] = dk.astype(BF16).reshape(4, 128, 128)
            dkv[1, cam, at] = dv.astype(BF16).reshape(4, 128, 128)
            return carry

        lax.fori_loop(2 * cam, 2 * cam + 2, step, 0)
        for k in range(4):
            drings[cam].sib_send(k)

    def query_back(cam):
        def step(c, carry):
            acc[...] += tn(keys(0, c), ds_buf[chunk(c), :])
            return carry

        lax.fori_loop(2 * cam, 2 * cam + 2, step, 0)

    def merge_query(pair):
        p_cp(pair, 0).wait_recv()
        Q[2 * pair : 2 * pair + 2] = whole(pair, 0)

    z_open(0)
    z_open(1)
    z_step(0, 1)
    z_open(2)
    z_step(0, 2)
    z_step(1, 1)
    relay_on(1)
    wring.first()
    z_step(0, 3)
    z_step(2, 1)
    relay_on(2)
    z_step(0, 4)
    z_step(1, 2)
    relay_on(3)
    z_step(2, 2)
    relay_on(4)
    wring.second()
    z_step(1, 3)
    wring.finish()
    z_step(2, 3)
    relay_end()
    project(0)
    z_step(1, 4)
    z_step(2, 4)
    merge(0)
    kvrings[0].start()
    project(1)
    kvrings[0].first()
    kvrings[0].second()
    merge_query(0)
    do_copy.wait_recv()
    kvrings[0].finish()
    forward(0, 1, 0)
    merge(1)
    kvrings[1].start()
    merge_query(1)
    forward(1, 2, 0)
    kvrings[1].first()
    kvrings[1].second()
    kvrings[1].finish()
    forward(0, 2, 1)
    inv, delta = settle()
    def shifted(k):
        return lax.rem(x + (2, 1, 3, 0)[k], 4)

    def make_dring(p):
        return RingScatter(
            pc,
            lambda k, half: dkv[half, p, 2 * shifted(k) + core].astype(F32),
            lambda k: dkv.at[:, p, 2 * shifted(k) + 1 - core],
            sib1.at[p], b1s.at[p], b1r.at[p], d_s.at[p], d_r.at[p],
        )

    drings = [make_dring(p) for p in range(4)]
    own_cols = lanes(v * 128, 128)

    def g_at(p, m, head):
        return G.at[pl.ds(128 * p, 128), lanes(m * 256 + head * 128, 128)]

    def g_copy(p, m, head):
        ref = g_at(p, m, head)
        return rcopy(ref, ref, e_s.at[p, m], e_r.at[p, m], pc.V)

    def give(p, m, value):
        g_at(p, m, v)[...] = value
        go(g_copy(p, m, v))

    def take(p):
        for cam in (2 * p, 2 * p + 1):
            for m in range(3):
                g_copy(cam, m, 1 - v).wait_recv()

    def hand_on(p):
        for half in range(2):
            give(p, 1 + half, drings[p].last(half).astype(BF16))

    back(0)
    go(rcopy(att.at[pl.ds(2 - 2 * v, 2)], att_out.at[:, :, own_cols], a_s, a_r, pc.V))
    back(1)
    drings[0].far()
    drings[0].near()
    back(2)
    drings[1].far()
    drings[1].near()
    drings[0].near2()
    back(3)
    drings[2].far()
    drings[2].near()
    drings[1].near2()
    hand_on(0)
    query_back(0)
    query_back(1)
    drings[3].far()
    drings[3].near()
    drings[2].near2()
    hand_on(1)
    query_back(2)
    query_back(3)
    drings[3].near2()
    hand_on(2)
    dq = jnp.transpose(acc[...] * SCALE).astype(BF16)
    for p in range(4):
        give(p, 0, dq[128 * p : 128 * p + 128])
    hand_on(3)
    att_out[:, :, own_cols] = att[pl.ds(2 * v, 2)]

    def token_term(pair):
        rows = G[256 * pair : 256 * pair + 256, :]

        def some(i, carry):
            acc = jnp.zeros((256, 640), F32)
            for m in range(3):
                weight = W[m, pl.ds(2 * i, 2)].reshape(640, 256)
                acc = acc + lax.dot_general(
                    rows[:, 256 * m : 256 * m + 256], weight, (((1,), (1,)), ((), ())),
                    preferred_element_type=F32,
                )
            TG[2 * pair : 2 * pair + 2, :, :, lanes(i * 640, 640)] = acc.reshape(2, 8, 16, 640)
            return carry

        lax.fori_loop(0, 4, some, 0)

    def t_steps(d, cam):
        return 4 if (d == 0) == (cam < 2) else 3

    def t_z_cp(d, s, cam):
        return rcopy(
            zbs.at[d, s - 1, cam], zbr.at[d, s - 1, cam], t_s.at[d, s - 1, cam], t_r.at[d, s - 1, cam],
            pc.ZP if d == 0 else pc.ZM,
        )

    def t_z_step(pair, s):
        for cam in (2 * pair, 2 * pair + 1):
            for d in range(2):
                n = t_steps(d, cam)
                if s <= n:
                    far = n - s + 1
                    value = TG[cam, lax.rem(z + (far if d == 0 else 8 - far), 8)]
                    if s > 1:
                        t_z_cp(d, s - 1, cam).wait_recv()
                        value = value + zbr[d, s - 2, cam].astype(F32)
                    zbs[d, s - 1, cam] = value.astype(BF16)
                    go(t_z_cp(d, s, cam))

    def t_z_last(pair):
        for cam in (2 * pair, 2 * pair + 1):
            value = TG[cam, z]
            for d in range(2):
                n = t_steps(d, cam)
                t_z_cp(d, n, cam).wait_recv()
                value = value + zbr[d, n - 1, cam].astype(F32)
            fin[cam] = value

    def g_own(k, half):
        return wt[k, :, pl.ds(half * 160, 160)]

    gring = RingScatter(pc, g_own, lambda k: sib2s.at[k], sib2r, b2s, b2r, f_s, f_r)

    def weight_term(k):
        cols = X[:, :, :, lanes(shifted(k) * 640, 640)].reshape(ROWS, 640)
        for m in range(3):
            acc = lax.dot_general(
                cols, G[:, 256 * m : 256 * m + 256], (((0,), (0,)), ((), ())),
                preferred_element_type=F32,
            )
            low, high = acc[:320], acc[320:]
            wt[k, m] = jnp.where(core == 0, low, high)
            other = jnp.where(core == 0, high, low).astype(BF16)
            sib2s[k, 0, m] = other[:160]
            sib2s[k, 1, m] = other[160:]
        gring.sib_send(k)

    take(0)
    token_term(0)
    t_z_step(0, 1)
    take(1)
    token_term(1)
    t_z_step(1, 1)
    weight_term(0)
    weight_term(1)
    t_z_step(0, 2)
    gring.far()
    weight_term(2)
    t_z_step(1, 2)
    gring.near()
    weight_term(3)
    t_z_step(0, 3)
    t_z_step(1, 3)
    gring.near2()
    t_z_step(0, 4)
    t_z_step(1, 4)
    for half in range(2):
        value = gring.last(half)
        rows = slice(160 * half, 160 * half + 160)
        for m, out in enumerate((gq, gk, gv)):
            out[rows] = value[m].astype(BF16)
    t_z_last(0)
    t_z_last(1)

    def piece(vv, yy):
        rows = pl.ds(pl.multiple_of(8 * yy, 8), 8)
        return jnp.concatenate((fin[2 * vv, rows], fin[2 * vv + 1, rows]), axis=0)

    def y_cp(k):
        return rcopy(ys.at[k], yr.at[k], y_s.at[k], y_r.at[k], (pc.V, pc.Y, pc.D)[k])

    for k, (vv, yy) in enumerate(((1 - v, y), (v, 1 - y), (1 - v, 1 - y))):
        ys[k] = piece(vv, yy).astype(BF16)
        go(y_cp(k))
    for k in range(3):
        y_cp(k).wait_recv()
    tgrad[:, lanes(v * HALF, HALF)] = (piece(v, y) + yr[1].astype(F32)).astype(BF16)
    tgrad[:, lanes((1 - v) * HALF, HALF)] = (yr[0].astype(F32) + yr[2].astype(F32)).astype(BF16)
    rcopy(att.at[pl.ds(2 - 2 * v, 2)], att_out.at[:, :, lanes((1 - v) * 128, 128)], a_s, a_r, pc.V).wait_recv()
    for ring in (wring, *kvrings, *drings, gring):
        ring.end()
    for c in (*swaps, do_copy, *sent):
        c.wait_send()


def hand_over_kernel(*refs):
    ins, outs, held, sems = refs[:5], refs[5:10], refs[10:15], refs[15]
    loads = [pltpu.make_async_copy(ins[i], held[i], sems.at[0, i]) for i in range(5)]
    stores = [pltpu.make_async_copy(held[i], outs[i], sems.at[1, i]) for i in range(5)]
    for c in loads:
        c.start()
    for load, store in zip(loads, stores):
        load.wait()
        store.start()
    for c in stores:
        c.wait()


def on_device(tokens, query_weight, key_weight, value_weight, out_grad, pairs, block_masks):
    vm = pl.BlockSpec(memory_space=pltpu.VMEM)
    sm = pl.BlockSpec(memory_space=pltpu.SMEM)
    hbm = pl.BlockSpec(memory_space=pl.ANY)
    dma = pltpu.SemaphoreType.DMA

    def shape(*dims):
        return jax.ShapeDtypeStruct(dims, BF16)

    def half(*dims):
        return pltpu.VMEM(dims, BF16)

    def full(*dims):
        return pltpu.VMEM(dims, F32)

    outs = pl.pallas_call(
        fused_kernel,
        out_shape=(
            shape(2, 128, 256), shape(16, 2 * HALF), shape(320, 256), shape(320, 256), shape(320, 256),
        ),
        in_specs=[vm] * 5 + [sm] * 2,
        out_specs=[vm] * 5,
        scratch_shapes=[
            half(4, 8, 16, HALF), half(3, 8, 320, 256), half(4, 128, 128), half(4, 128, 128),
            half(2, 4, 8, 128, 128), half(2, 2, 16, HALF), full(2, 3, 256, 128),
            half(2, 3, 256, 128), half(2, 3, 256, 128), half(2, 4, 16, HALF),
            full(8, ROWS), full(4, 16, ROWS), full(4096, ROWS), half(4096, ROWS),
            full(16, ROWS), full(8, ROWS),
            full(128, ROWS), half(4, 128, 128), half(2, 4, 8, 128, 128),
            half(ROWS, 768), full(4, 8, 16, HALF), half(2, 4, 4, 16, HALF), half(2, 4, 4, 16, HALF),
            full(4, 16, HALF), half(3, 16, HALF), half(3, 16, HALF),
            half(4, 4, 2, 128, 128), half(4, 6, 128, 128), half(4, 6, 128, 128),
            full(4, 3, 320, 256), half(4, 2, 3, 160, 256), half(4, 2, 3, 160, 256),
            half(6, 3, 160, 256), half(6, 3, 160, 256),
            dma((3,)), dma((3,)), dma, dma, dma((2, 4, 3)), dma((2, 4, 3)),
            dma((14,)), dma((14,)), dma((2, 14)), dma((2, 14)), dma((2, 2)), dma((2, 2)),
            dma((2, 2, 4)), dma((2, 2, 4)),
            dma, dma, dma((4, 3)), dma((4, 3)), dma((2, 4, 4)), dma((2, 4, 4)), dma((3,)), dma((3,)),
            dma((4, 10)), dma((4, 10)), dma((10,)), dma((10,)),
        ],
        compiler_params=pltpu.CompilerParams(
            collective_id=0, has_side_effects=True, vmem_limit_bytes=VMEM_LIMIT
        ),
        name="fused",
    )(
        tokens.reshape(16, 2 * HALF), query_weight, key_weight, value_weight, out_grad, pairs.T,
        block_masks,
    )

    att_out, tgrad, gq, gk, gv = pl.pallas_call(
        hand_over_kernel,
        out_shape=tuple(jax.ShapeDtypeStruct(a.shape, a.dtype) for a in outs),
        in_specs=[hbm] * 5,
        out_specs=[hbm] * 5,
        scratch_shapes=[*(pltpu.VMEM(a.shape, BF16) for a in outs), dma((2, 5))],
        compiler_params=pltpu.CompilerParams(vmem_limit_bytes=VMEM_LIMIT),
        name="hand_over",
    )(*outs)
    return (att_out, tgrad.reshape(2, 8, 2 * HALF), gq, gk, gv)


def solution(mesh):
    return jax.shard_map(
        on_device,
        mesh=mesh,
        in_specs=(
            P("view", ("tm", "head"), None),
            P(("view", "tm"), "head"),
            P(("view", "tm"), "head"),
            P(("view", "tm"), "head"),
            P("view", "tm", "head"),
            P(),
            P(),
        ),
        out_specs=(
            P("view", "tm", "head"),
            P("view", ("tm", "head"), None),
            P(("view", "tm"), "head"),
            P(("view", "tm"), "head"),
            P(("view", "tm"), "head"),
        ),
        check_vma=False,
    )
```

time: 158 us -> 127 us (0.80)
  Pallas kernels: 147 us -> 126 us
  local copies, waits for them, and re-layouts: 9.29 us -> 0 us
    pallas_call x3 -> x2, Pallas kernels: 147 us -> 126 us  [the longest x1 124 us: on_device(): pl.pallas_call(fused_kernel, out_shape=(shape(2, 128, 256), shape(16, 2 *...]
    unnamed x6 -> x0, local copies, waits for them, and re-layouts: 9.29 us -> none
where the time goes in v2:
time: 127 us
  Pallas kernels  126 us (99%)
    pallas_call x1, Pallas kernels, on_device(): pl.pallas_call(fused_kernel, out_shape=(shape(2, 128, 256), shape(16, 2 *...  124 us

profile of v2, /device:TPU:2, one launch (start us, length us, event | category | flops | bytes accessed | tf_op | source)
XLA Modules:
  0.0 126.7 jit_solution(10606469664339006731)
XLA Ops:
  0.6 123.9 %fused.1 = (bf16[2,128,256]{2,1,0:T(8,128)(2,1)}, bf16[16,5120]{1,0:T(8,128)(2,1)}, bf16[320,256]{1,0:T(8,128)(2,1)}, bf16[320,256]{1,0:T(8,128)(2,1)}, bf16[320,256]{1,0:T(8,128)(2,1)}) custom-call(bf16[16,5120]{1,0:T(8,128)(2,1)} %bitcast.3, bf16[320,256]{1,0:T(8,128)(2,1)} %wq.1, bf16[320,256]{1,0:T(8,128)(2,1)} %wk.1, bf16[320,256]{1,0:T(8,128)(2,1)} %wv.1, ...), custom_call_target="tpu_custom_call" | custom-call | tf_op jit(solution)/shard_map/fused/pallas_call | solution.py:652
  124.6 2.0 %hand_over.1 = (bf16[2,128,256]{2,1,0:T(8,128)(2,1)}, bf16[16,5120]{1,0:T(8,128)(2,1)}, bf16[320,256]{1,0:T(8,128)(2,1)}, bf16[320,256]{1,0:T(8,128)(2,1)}, bf16[320,256]{1,0:T(8,128)(2,1)}) custom-call(bf16[2,128,256]{2,1,0:T(8,128)(2,1)} %get-tuple-element.15.refs_0_, bf16[16,5120]{1,0:T(8,128)(2,1)} %get-tuple-element.16.refs_1_, ...), custom_call_target="tpu_custom_call" | custom-call | tf_op jit(solution)/shard_map/hand_over/pallas_call | solution.py:686

commit v3 on v2

--- a/solution.py
+++ b/solution.py
@@ -16,7 +16,6 @@
 ROWS = 512
 SCALE = 1.0 / math.sqrt(128)
 CLOSED = -1e30
-Z_STEPS = ((4, 3), (3, 4), (4, 3))
 LOG2E = math.log2(math.e)
 
 
@@ -178,35 +177,45 @@
 def fused_kernel(
     tok, wq, wk, wv, dout, pairs, masks,
     att_out, tgrad, gq, gk, gv,
-    X, W, Q, DO, KV, stage, kept, part_s, part_r, relay,
+    X, W, Q, DO, KV, stage, kept, part_s, part_r,
     link, bias, s_buf, ds_buf, tops, stat, acc, att, dkv,
     G, TG, zbs, zbr, fin, ys, yr, sib1, b1s, b1r, wt, sib2s, sib2r, b2s, b2r,
-    sw_s, sw_r, do_s, do_r, z_s, z_r, w_s, w_r, k_s, k_r, p_s, p_r, r_s, r_r,
+    l_s, sw_s, sw_r, do_s, do_r, z_s, z_r, w_s, w_r, k_s, k_r, p_s, p_r,
     a_s, a_r, e_s, e_r, t_s, t_r, y_s, y_r, d_s, d_r, f_s, f_r,
 ):
     pc = Place()
     v, t, z, y, x, core = pc.v, pc.t, pc.z, pc.y, pc.x, pc.core
+    loads = [
+        pltpu.make_async_copy(tok.at[:, lanes(v * HALF, HALF)], stage.at[v, y], l_s.at[0]),
+        pltpu.make_async_copy(wq, W.at[0, t], l_s.at[1]),
+        pltpu.make_async_copy(wk, W.at[1, t], l_s.at[2]),
+        pltpu.make_async_copy(wv, W.at[2, t], l_s.at[3]),
+        pltpu.make_async_copy(
+            dout.at[:, :, lanes(v * 128, 128)], DO.at[pl.ds(2 * v, 2)], l_s.at[4]
+        ),
+    ]
+    for c in loads:
+        c.start()
     pc.greet()
     swaps = []
-    for k, (dev, vv) in enumerate(((pc.V, 1 - v), (pc.Y, v), (pc.D, 1 - v))):
+    sent = []
+    y2 = 1 - y
+    for k, dev, vv in ((0, pc.V, 1 - v), (2, pc.D, 1 - v), (1, pc.Y, v)):
         c = rcopy(tok.at[:, lanes(vv * HALF, HALF)], stage.at[v, y], sw_s.at[k], sw_r.at[k], dev)
         c.start()
         swaps.append(c)
-    W[0, t] = wq[...]
-    W[1, t] = wk[...]
-    W[2, t] = wv[...]
 
     def w_at(tt, half):
         return W.at[:, tt, pl.ds(half * 160, 160)]
 
+    for c in loads:
+        c.wait()
     wring = RingGather(pc, w_at, w_s, w_r)
     wring.start()
-    stage[v, y] = tok[:, lanes(v * HALF, HALF)]
     do_copy = rcopy(
         dout.at[:, :, lanes((1 - v) * 128, 128)], DO.at[pl.ds(2 * v, 2)], do_s, do_r, pc.V
     )
     do_copy.start()
-    DO[pl.ds(2 * v, 2)] = dout[:, :, lanes(v * 128, 128)]
 
     def make_bias():
         for j in range(4):
@@ -226,65 +235,40 @@
                 bias[j, pl.ds(s, 1), :] = link[pl.ds(j, 1), :] + level
 
     make_bias()
-    y2 = 1 - y
-    for k, (a, b) in enumerate(((1 - v, y), (v, y2), (1 - v, y2))):
+
+    def swapped(k, a, b):
         rcopy(stage.at[a, b], stage.at[a, b], sw_s.at[k], sw_r.at[k], pc.V).wait_recv()
-    for vv in range(2):
+
+    def assemble(vv):
         low = stage[vv, 0].astype(F32)
         high = stage[vv, 1].astype(F32)
         for c in range(2):
             both = jnp.concatenate((low[8 * c : 8 * c + 8], high[8 * c : 8 * c + 8]), axis=0)
             X[2 * vv + c, z] = both.astype(BF16)
 
-    sent = []
-    cam_of = (y, 2, 3)
-
-    def z_block(d, s):
-        return lax.rem(z + ((8 - s) if d == 0 else s), 8)
-
-    def z_cp(d, s, u):
-        ref = X.at[cam_of[u], z_block(d, s - 1)]
-        return rcopy(
-            ref, ref, z_s.at[d, s - 1, u], z_r.at[d, s - 1, u], pc.ZP if d == 0 else pc.ZM
-        )
-
-    def z_send(d, s, u):
-        c = z_cp(d, s, u)
-        c.start()
-        sent.append(c)
-
-    def z_open(u):
-        for d in range(2):
-            z_send(d, 1, u)
-
-    def z_step(u, s):
-        for d in range(2):
-            if s <= Z_STEPS[u][d]:
-                ref = X.at[cam_of[u], z_block(d, s)]
-                rcopy(ref, ref, z_s.at[d, s - 1, u], z_r.at[d, s - 1, u], pc.ZP).wait_recv()
-                if s < Z_STEPS[u][d]:
-                    z_send(d, s + 1, u)
-                if u == 0:
-                    c = rcopy(ref, relay.at[d, s - 1], r_s.at[0, d, s - 1], r_r.at[0, d, s - 1], pc.V)
-                    c.start()
-                    sent.append(c)
-
-    def relay_on(s):
-        for d in range(2):
-            if s <= Z_STEPS[0][d]:
-                ref = relay.at[d, s - 1]
-                rcopy(ref, ref, r_s.at[0, d, s - 1], r_r.at[0, d, s - 1], pc.V).wait_recv()
-                there = X.at[y, z_block(d, s)]
-                c = rcopy(ref, there, r_s.at[1, d, s - 1], r_r.at[1, d, s - 1], pc.D)
-                c.start()
-                sent.append(c)
-
-    def relay_end():
-        for s in range(1, 5):
+    def steps(d, cam):
+        return 4 if (d == 0) == (cam < 2) else 3
+
+    def z_ref(d, s, cam):
+        return X.at[cam, lax.rem(z + ((8 - s) if d == 0 else s), 8)]
+
+    def z_send(d, s, cam):
+        ref = z_ref(d, s - 1, cam)
+        go(rcopy(ref, ref, z_s.at[d, s - 1, cam], z_r.at[d, s - 1, cam], pc.ZP if d == 0 else pc.ZM))
+
+    def z_open(pair):
+        for cam in (2 * pair, 2 * pair + 1):
             for d in range(2):
-                if s <= Z_STEPS[0][d]:
-                    ref = X.at[1 - y, z_block(d, s)]
-                    rcopy(ref, ref, r_s.at[1, d, s - 1], r_r.at[1, d, s - 1], pc.D).wait_recv()
+                z_send(d, 1, cam)
+
+    def z_step(pair, s):
+        for cam in (2 * pair, 2 * pair + 1):
+            for d in range(2):
+                if s <= steps(d, cam):
+                    ref = z_ref(d, s, cam)
+                    rcopy(ref, ref, z_s.at[d, s - 1, cam], z_r.at[d, s - 1, cam], pc.ZP).wait_recv()
+                    if s < steps(d, cam):
+                        z_send(d, s + 1, cam)
 
     def go(c):
         c.start()
@@ -301,28 +285,34 @@
             return carry
 
         lax.fori_loop(1, 3, one, 0)
-        go(p_cp(pair, 1))
+        go(p_cp(2 * pair, 1))
+        go(p_cp(2 * pair + 1, 1))
         lax.fori_loop(0, 1, one, 0)
-        go(p_cp(pair, 0))
-
-    def p_cp(pair, i):
-        part = pl.ds(0, 1) if i == 0 else pl.ds(1, 2)
-        return rcopy(
-            part_s.at[pair, part], part_r.at[pair, part], p_s.at[pair, i], p_r.at[pair, i], pc.V
-        )
-
-    def whole(pair, m):
-        return (kept[pair, m] + part_r[pair, m].astype(F32)).astype(BF16).reshape(2, 128, 128)
-
-    def merge(pair):
-        p_cp(pair, 1).wait_recv()
+        go(p_cp(2 * pair, 0))
+        go(p_cp(2 * pair + 1, 0))
+
+    def p_cp(cam, i):
+        at = (cam // 2, pl.ds(0, 1) if i == 0 else pl.ds(1, 2), pl.ds(128 * (cam % 2), 128))
+        return rcopy(part_s.at[at], part_r.at[at], p_s.at[cam, i], p_r.at[cam, i], pc.V)
+
+    def whole(cam, m):
+        at = (cam // 2, m, pl.ds(128 * (cam % 2), 128))
+        return (kept[at] + part_r[at].astype(F32)).astype(BF16)
+
+    def merge(cam):
+        p_cp(cam, 1).wait_recv()
         for m in (1, 2):
-            KV[m - 1, 2 * pair : 2 * pair + 2, t] = whole(pair, m)
-
-    def kv_at(pair):
-        return lambda tt, half: KV.at[half, pl.ds(2 * pair, 2), tt]
-
-    kvrings = [RingGather(pc, kv_at(p), k_s.at[p], k_r.at[p]) for p in range(2)]
+            KV[m - 1, cam, t] = whole(cam, m)
+        kvrings[cam].start()
+
+    def merge_query(cam):
+        p_cp(cam, 0).wait_recv()
+        Q[cam] = whole(cam, 0)
+
+    def kv_at(cam):
+        return lambda tt, half: KV.at[half, cam, tt]
+
+    kvrings = [RingGather(pc, kv_at(c), k_s.at[c], k_r.at[c]) for c in range(4)]
 
     def nt(a, b):
         return lax.dot_general(a, b, (((1,), (1,)), ((), ())), preferred_element_type=F32)
@@ -397,50 +387,49 @@
 
         lax.fori_loop(2 * cam, 2 * cam + 2, step, 0)
 
-    def merge_query(pair):
-        p_cp(pair, 0).wait_recv()
-        Q[2 * pair : 2 * pair + 2] = whole(pair, 0)
-
-    z_open(0)
-    z_open(1)
+    swapped(0, 1 - v, y)
+    swapped(2, 1 - v, y2)
+    assemble(1 - v)
+    z_open(1 - v)
+    swapped(1, v, y2)
+    assemble(v)
+    z_open(v)
     z_step(0, 1)
-    z_open(2)
+    z_step(1, 1)
     z_step(0, 2)
-    z_step(1, 1)
-    relay_on(1)
     wring.first()
+    z_step(1, 2)
     z_step(0, 3)
-    z_step(2, 1)
-    relay_on(2)
-    z_step(0, 4)
-    z_step(1, 2)
-    relay_on(3)
-    z_step(2, 2)
-    relay_on(4)
     wring.second()
     z_step(1, 3)
+    z_step(0, 4)
     wring.finish()
-    z_step(2, 3)
-    relay_end()
     project(0)
     z_step(1, 4)
-    z_step(2, 4)
+    project(1)
     merge(0)
-    kvrings[0].start()
-    project(1)
+    merge(1)
     kvrings[0].first()
+    kvrings[1].first()
+    merge(2)
+    merge(3)
     kvrings[0].second()
+    kvrings[1].second()
     merge_query(0)
+    merge_query(1)
     do_copy.wait_recv()
     kvrings[0].finish()
+    kvrings[1].finish()
+    kvrings[2].first()
+    kvrings[3].first()
     forward(0, 1, 0)
-    merge(1)
-    kvrings[1].start()
-    merge_query(1)
+    kvrings[2].second()
+    kvrings[3].second()
+    merge_query(2)
+    merge_query(3)
     forward(1, 2, 0)
-    kvrings[1].first()
-    kvrings[1].second()
-    kvrings[1].finish()
+    kvrings[2].finish()
+    kvrings[3].finish()
     forward(0, 2, 1)
     inv, delta = settle()
     def shifted(k):
@@ -457,74 +446,58 @@
     drings = [make_dring(p) for p in range(4)]
     own_cols = lanes(v * 128, 128)
 
-    def g_at(p, m, head):
-        return G.at[pl.ds(128 * p, 128), lanes(m * 256 + head * 128, 128)]
-
     def g_copy(p, m, head):
-        ref = g_at(p, m, head)
-        return rcopy(ref, ref, e_s.at[p, m], e_r.at[p, m], pc.V)
+        rows = pl.ds(0, ROWS) if m == 0 else pl.ds(128 * p, 128)
+        ref = G.at[rows, lanes(m * 256 + head * 128, 128)]
+        return ref, rcopy(ref, ref, e_s.at[p, m], e_r.at[p, m], pc.V)
 
     def give(p, m, value):
-        g_at(p, m, v)[...] = value
-        go(g_copy(p, m, v))
-
-    def take(p):
-        for cam in (2 * p, 2 * p + 1):
-            for m in range(3):
-                g_copy(cam, m, 1 - v).wait_recv()
+        ref, c = g_copy(p, m, v)
+        ref[...] = value
+        go(c)
+
+    def take(p, m):
+        g_copy(p, m, 1 - v)[1].wait_recv()
 
     def hand_on(p):
         for half in range(2):
             give(p, 1 + half, drings[p].last(half).astype(BF16))
 
     back(0)
-    go(rcopy(att.at[pl.ds(2 - 2 * v, 2)], att_out.at[:, :, own_cols], a_s, a_r, pc.V))
     back(1)
     drings[0].far()
     drings[0].near()
     back(2)
+    back(3)
+    drings[0].near2()
     drings[1].far()
     drings[1].near()
-    drings[0].near2()
-    back(3)
+    for cam in range(4):
+        query_back(cam)
+    give(0, 0, jnp.transpose(acc[...] * SCALE).astype(BF16))
+    drings[1].near2()
+    hand_on(0)
     drings[2].far()
     drings[2].near()
-    drings[1].near2()
-    hand_on(0)
-    query_back(0)
-    query_back(1)
     drings[3].far()
     drings[3].near()
+    hand_on(1)
     drings[2].near2()
-    hand_on(1)
-    query_back(2)
-    query_back(3)
     drings[3].near2()
-    hand_on(2)
-    dq = jnp.transpose(acc[...] * SCALE).astype(BF16)
-    for p in range(4):
-        give(p, 0, dq[128 * p : 128 * p + 128])
-    hand_on(3)
     att_out[:, :, own_cols] = att[pl.ds(2 * v, 2)]
 
-    def token_term(pair):
-        rows = G[256 * pair : 256 * pair + 256, :]
+    def token_term(cam, n):
+        rows = G[128 * cam : 128 * (cam + n), :]
 
         def some(i, carry):
-            acc = jnp.zeros((256, 640), F32)
+            total = jnp.zeros((128 * n, 640), F32)
             for m in range(3):
                 weight = W[m, pl.ds(2 * i, 2)].reshape(640, 256)
-                acc = acc + lax.dot_general(
-                    rows[:, 256 * m : 256 * m + 256], weight, (((1,), (1,)), ((), ())),
-                    preferred_element_type=F32,
-                )
-            TG[2 * pair : 2 * pair + 2, :, :, lanes(i * 640, 640)] = acc.reshape(2, 8, 16, 640)
+                total = total + nt(rows[:, 256 * m : 256 * m + 256], weight)
+            TG[cam : cam + n, :, :, lanes(i * 640, 640)] = total.reshape(n, 8, 16, 640)
             return carry
 
         lax.fori_loop(0, 4, some, 0)
-
-    def t_steps(d, cam):
-        return 4 if (d == 0) == (cam < 2) else 3
 
     def t_z_cp(d, s, cam):
         return rcopy(
@@ -532,73 +505,94 @@
             pc.ZP if d == 0 else pc.ZM,
         )
 
-    def t_z_step(pair, s):
-        for cam in (2 * pair, 2 * pair + 1):
-            for d in range(2):
-                n = t_steps(d, cam)
-                if s <= n:
-                    far = n - s + 1
-                    value = TG[cam, lax.rem(z + (far if d == 0 else 8 - far), 8)]
-                    if s > 1:
-                        t_z_cp(d, s - 1, cam).wait_recv()
-                        value = value + zbr[d, s - 2, cam].astype(F32)
-                    zbs[d, s - 1, cam] = value.astype(BF16)
-                    go(t_z_cp(d, s, cam))
-
-    def t_z_last(pair):
-        for cam in (2 * pair, 2 * pair + 1):
-            value = TG[cam, z]
-            for d in range(2):
-                n = t_steps(d, cam)
-                t_z_cp(d, n, cam).wait_recv()
-                value = value + zbr[d, n - 1, cam].astype(F32)
-            fin[cam] = value
-
-    def g_own(k, half):
-        return wt[k, :, pl.ds(half * 160, 160)]
-
-    gring = RingScatter(pc, g_own, lambda k: sib2s.at[k], sib2r, b2s, b2r, f_s, f_r)
-
-    def weight_term(k):
-        cols = X[:, :, :, lanes(shifted(k) * 640, 640)].reshape(ROWS, 640)
-        for m in range(3):
-            acc = lax.dot_general(
-                cols, G[:, 256 * m : 256 * m + 256], (((0,), (0,)), ((), ())),
-                preferred_element_type=F32,
-            )
-            low, high = acc[:320], acc[320:]
-            wt[k, m] = jnp.where(core == 0, low, high)
+    def t_step(cam, s):
+        for d in range(2):
+            n = steps(d, cam)
+            if s <= n:
+                far = n - s + 1
+                value = TG[cam, lax.rem(z + (far if d == 0 else 8 - far), 8)]
+                if s > 1:
+                    t_z_cp(d, s - 1, cam).wait_recv()
+                    value = value + zbr[d, s - 2, cam].astype(F32)
+                zbs[d, s - 1, cam] = value.astype(BF16)
+                go(t_z_cp(d, s, cam))
+
+    def t_last(cam):
+        value = TG[cam, z]
+        for d in range(2):
+            n = steps(d, cam)
+            t_z_cp(d, n, cam).wait_recv()
+            value = value + zbr[d, n - 1, cam].astype(F32)
+        fin[cam] = value
+
+    def make_gring(m):
+        return RingScatter(
+            pc,
+            lambda k, half: wt[m, k, pl.ds(half * 160, 160)],
+            lambda k: sib2s.at[m, k],
+            sib2r.at[m], b2s.at[m], b2r.at[m], f_s.at[m], f_r.at[m],
+        )
+
+    grings = [make_gring(m) for m in range(3)]
+
+    def weight_term(m):
+        for k in range(4):
+            cols = X[:, :, :, lanes(shifted(k) * 640, 640)].reshape(ROWS, 640)
+            term = tn(cols, G[:, 256 * m : 256 * m + 256])
+            low, high = term[:320], term[320:]
+            wt[m, k] = jnp.where(core == 0, low, high)
             other = jnp.where(core == 0, high, low).astype(BF16)
-            sib2s[k, 0, m] = other[:160]
-            sib2s[k, 1, m] = other[160:]
-        gring.sib_send(k)
-
-    take(0)
-    token_term(0)
-    t_z_step(0, 1)
-    take(1)
-    token_term(1)
-    t_z_step(1, 1)
+            sib2s[m, k, 0] = other[:160]
+            sib2s[m, k, 1] = other[160:]
+            grings[m].sib_send(k)
+
+    def token_start(cam, n):
+        for c in range(cam, cam + n):
+            take(c, 1)
+            take(c, 2)
+        token_term(cam, n)
+        for c in range(cam, cam + n):
+            t_step(c, 1)
+
+    def weight_out(m, out):
+        for half in range(2):
+            out[160 * half : 160 * half + 160] = grings[m].last(half).astype(BF16)
+
+    take(0, 0)
+    token_start(0, 1)
+    hand_on(2)
+    token_start(1, 1)
+    hand_on(3)
+    go(rcopy(att.at[pl.ds(2 - 2 * v, 2)], att_out.at[:, :, own_cols], a_s, a_r, pc.V))
+    t_step(0, 2)
+    t_step(1, 2)
+    token_start(2, 2)
     weight_term(0)
+    t_step(0, 3)
+    t_step(1, 3)
+    grings[0].far()
     weight_term(1)
-    t_z_step(0, 2)
-    gring.far()
+    t_step(2, 2)
+    t_step(3, 2)
+    grings[0].near()
     weight_term(2)
-    t_z_step(1, 2)
-    gring.near()
-    weight_term(3)
-    t_z_step(0, 3)
-    t_z_step(1, 3)
-    gring.near2()
-    t_z_step(0, 4)
-    t_z_step(1, 4)
-    for half in range(2):
-        value = gring.last(half)
-        rows = slice(160 * half, 160 * half + 160)
-        for m, out in enumerate((gq, gk, gv)):
-            out[rows] = value[m].astype(BF16)
-    t_z_last(0)
-    t_z_last(1)
+    t_step(0, 4)
+    t_step(1, 4)
+    grings[1].far()
+    grings[1].near()
+    grings[0].near2()
+    t_step(2, 3)
+    t_step(3, 3)
+    grings[2].far()
+    grings[2].near()
+    grings[1].near2()
+    weight_out(0, gq)
+    t_step(2, 4)
+    t_step(3, 4)
+    grings[2].near2()
+    weight_out(1, gk)
+    for cam in range(4):
+        t_last(cam)
 
     def piece(vv, yy):
         rows = pl.ds(pl.multiple_of(8 * yy, 8), 8)
@@ -610,12 +604,13 @@
     for k, (vv, yy) in enumerate(((1 - v, y), (v, 1 - y), (1 - v, 1 - y))):
         ys[k] = piece(vv, yy).astype(BF16)
         go(y_cp(k))
+    weight_out(2, gv)
     for k in range(3):
         y_cp(k).wait_recv()
     tgrad[:, lanes(v * HALF, HALF)] = (piece(v, y) + yr[1].astype(F32)).astype(BF16)
     tgrad[:, lanes((1 - v) * HALF, HALF)] = (yr[0].astype(F32) + yr[2].astype(F32)).astype(BF16)
     rcopy(att.at[pl.ds(2 - 2 * v, 2)], att_out.at[:, :, lanes((1 - v) * 128, 128)], a_s, a_r, pc.V).wait_recv()
-    for ring in (wring, *kvrings, *drings, gring):
+    for ring in (wring, *kvrings, *drings, *grings):
         ring.end()
     for c in (*swaps, do_copy, *sent):
         c.wait_send()
@@ -654,25 +649,24 @@
         out_shape=(
             shape(2, 128, 256), shape(16, 2 * HALF), shape(320, 256), shape(320, 256), shape(320, 256),
         ),
-        in_specs=[vm] * 5 + [sm] * 2,
+        in_specs=[hbm] * 5 + [sm] * 2,
         out_specs=[vm] * 5,
         scratch_shapes=[
             half(4, 8, 16, HALF), half(3, 8, 320, 256), half(4, 128, 128), half(4, 128, 128),
             half(2, 4, 8, 128, 128), half(2, 2, 16, HALF), full(2, 3, 256, 128),
-            half(2, 3, 256, 128), half(2, 3, 256, 128), half(2, 4, 16, HALF),
+            half(2, 3, 256, 128), half(2, 3, 256, 128),
             full(8, ROWS), full(4, 16, ROWS), full(4096, ROWS), half(4096, ROWS),
             full(16, ROWS), full(8, ROWS),
             full(128, ROWS), half(4, 128, 128), half(2, 4, 8, 128, 128),
             half(ROWS, 768), full(4, 8, 16, HALF), half(2, 4, 4, 16, HALF), half(2, 4, 4, 16, HALF),
             full(4, 16, HALF), half(3, 16, HALF), half(3, 16, HALF),
             half(4, 4, 2, 128, 128), half(4, 6, 128, 128), half(4, 6, 128, 128),
-            full(4, 3, 320, 256), half(4, 2, 3, 160, 256), half(4, 2, 3, 160, 256),
-            half(6, 3, 160, 256), half(6, 3, 160, 256),
-            dma((3,)), dma((3,)), dma, dma, dma((2, 4, 3)), dma((2, 4, 3)),
-            dma((14,)), dma((14,)), dma((2, 14)), dma((2, 14)), dma((2, 2)), dma((2, 2)),
-            dma((2, 2, 4)), dma((2, 2, 4)),
+            full(3, 4, 320, 256), half(3, 4, 2, 160, 256), half(3, 4, 2, 160, 256),
+            half(3, 6, 160, 256), half(3, 6, 160, 256),
+            dma((5,)), dma((3,)), dma((3,)), dma, dma, dma((2, 4, 4)), dma((2, 4, 4)),
+            dma((14,)), dma((14,)), dma((4, 14)), dma((4, 14)), dma((4, 2)), dma((4, 2)),
             dma, dma, dma((4, 3)), dma((4, 3)), dma((2, 4, 4)), dma((2, 4, 4)), dma((3,)), dma((3,)),
-            dma((4, 10)), dma((4, 10)), dma((10,)), dma((10,)),
+            dma((4, 10)), dma((4, 10)), dma((3, 10)), dma((3, 10)),
         ],
         compiler_params=pltpu.CompilerParams(
             collective_id=0, has_side_effects=True, vmem_limit_bytes=VMEM_LIMIT

time: 127 us -> 122 us (0.961)
  Pallas kernels: 126 us -> 121 us
    pallas_call x1, Pallas kernels: 124 us -> 119 us  [on_device(): pl.pallas_call(fused_kernel, out_shape=(shape(2, 128, 256), shape(16, 2 *...]
where the time goes in v3:
time: 122 us
  Pallas kernels  121 us (99%)
    pallas_call x1, Pallas kernels, on_device(): pl.pallas_call(fused_kernel, out_shape=(shape(2, 128, 256), shape(16, 2 *...  119 us

profile of v3, /device:TPU:2, one launch (start us, length us, event | category | flops | bytes accessed | tf_op | source)
XLA Modules:
  0.0 121.7 jit_solution(8496530834762198317)
XLA Ops:
  0.6 118.9 %fused.1 = (bf16[2,128,256]{2,1,0:T(8,128)(2,1)}, bf16[16,5120]{1,0:T(8,128)(2,1)}, bf16[320,256]{1,0:T(8,128)(2,1)}, bf16[320,256]{1,0:T(8,128)(2,1)}, bf16[320,256]{1,0:T(8,128)(2,1)}) custom-call(bf16[16,5120]{1,0:T(8,128)(2,1)} %bitcast.3, bf16[320,256]{1,0:T(8,128)(2,1)} %wq.1, bf16[320,256]{1,0:T(8,128)(2,1)} %wk.1, bf16[320,256]{1,0:T(8,128)(2,1)} %wv.1, ...), custom_call_target="tpu_custom_call" | custom-call | tf_op jit(solution)/shard_map/fused/pallas_call | solution.py:647
  119.5 2.0 %hand_over.1 = (bf16[2,128,256]{2,1,0:T(8,128)(2,1)}, bf16[16,5120]{1,0:T(8,128)(2,1)}, bf16[320,256]{1,0:T(8,128)(2,1)}, bf16[320,256]{1,0:T(8,128)(2,1)}, bf16[320,256]{1,0:T(8,128)(2,1)}) custom-call(bf16[2,128,256]{2,1,0:T(8,128)(2,1)} %get-tuple-element.15.refs_0_, bf16[16,5120]{1,0:T(8,128)(2,1)} %get-tuple-element.16.refs_1_, ...), custom_call_target="tpu_custom_call" | custom-call | tf_op jit(solution)/shard_map/hand_over/pallas_call | solution.py:680

commit v4 on v3

--- a/solution.py
+++ b/solution.py
@@ -321,10 +321,10 @@
         return lax.dot_general(a, b, (((0,), (0,)), ((), ())), preferred_element_type=F32)
 
     def keys(m, c):
-        return KV[m, c // 2, pl.ds(4 * lax.rem(c, 2), 4)].reshape(512, 128)
+        return KV[m, c].reshape(1024, 128)
 
     def chunk(c):
-        return pl.ds(pl.multiple_of(c * 512, 512), 512)
+        return pl.ds(pl.multiple_of(c * 1024, 1024), 1024)
 
     def forward(low, high, kp):
         qs = slice(256 * low, 256 * high)
@@ -333,9 +333,8 @@
         def step(c, carry):
             top, total = carry
             s = nt(keys(0, c), Q[2 * low : 2 * high].reshape(width, 128)) * (SCALE * LOG2E)
-            block = 8 * lax.rem(c, 2)
             parts = [
-                s[64 * e : 64 * e + 64] + bias[c // 2, pl.ds(block + e, 1), qs] for e in range(8)
+                s[64 * e : 64 * e + 64] + bias[c, pl.ds(e, 1), qs] for e in range(16)
             ]
             s = jnp.concatenate(parts, axis=0)
             new_top = jnp.maximum(top, jnp.max(s, axis=0, keepdims=True))
@@ -351,7 +350,7 @@
             acc[:, qs] = jnp.zeros((128, width), F32)
         else:
             start = (stat[0:1, qs], stat[1:2, qs])
-        top, total = lax.fori_loop(4 * kp, 4 * kp + 4, step, start)
+        top, total = lax.fori_loop(2 * kp, 2 * kp + 2, step, start)
         stat[0:1, qs] = top
         stat[1:2, qs] = total
 
@@ -360,7 +359,6 @@
         out = jnp.transpose(acc[...] * inv).astype(BF16)
         att[...] = out.reshape(4, 128, 128)
         prod = out.astype(F32) * DO[...].reshape(ROWS, 128).astype(F32)
-        acc[...] = jnp.zeros((128, ROWS), F32)
         return inv, jnp.sum(jnp.transpose(prod), axis=0, keepdims=True)
 
     def back(cam):
@@ -371,21 +369,19 @@
             ds = (w * (nt(keys(1, c), g) - delta)).astype(BF16)
             ds_buf[chunk(c), :] = ds
             dk = jnp.dot(ds, Q[...].reshape(ROWS, 128), preferred_element_type=F32) * SCALE
-            at = pl.ds(4 * lax.rem(c, 2), 4)
-            dkv[0, cam, at] = dk.astype(BF16).reshape(4, 128, 128)
-            dkv[1, cam, at] = dv.astype(BF16).reshape(4, 128, 128)
+            dkv[0, cam] = dk.astype(BF16).reshape(8, 128, 128)
+            dkv[1, cam] = dv.astype(BF16).reshape(8, 128, 128)
             return carry
 
-        lax.fori_loop(2 * cam, 2 * cam + 2, step, 0)
+        lax.fori_loop(cam, cam + 1, step, 0)
         for k in range(4):
             drings[cam].sib_send(k)
 
-    def query_back(cam):
-        def step(c, carry):
-            acc[...] += tn(keys(0, c), ds_buf[chunk(c), :])
-            return carry
-
-        lax.fori_loop(2 * cam, 2 * cam + 2, step, 0)
+    def query_back():
+        total = tn(keys(0, 0), ds_buf[chunk(0), :])
+        for c in range(1, 4):
+            total = total + tn(keys(0, c), ds_buf[chunk(c), :])
+        return jnp.transpose(total * SCALE).astype(BF16)
 
     swapped(0, 1 - v, y)
     swapped(2, 1 - v, y2)
@@ -472,9 +468,7 @@
     drings[0].near2()
     drings[1].far()
     drings[1].near()
-    for cam in range(4):
-        query_back(cam)
-    give(0, 0, jnp.transpose(acc[...] * SCALE).astype(BF16))
+    give(0, 0, query_back())
     drings[1].near2()
     hand_on(0)
     drings[2].far()

time: 122 us -> 120 us (0.984)
  Pallas kernels: 121 us -> 119 us
    pallas_call x1, Pallas kernels: 119 us -> 117 us  [on_device(): pl.pallas_call(fused_kernel, out_shape=(shape(2, 128, 256), shape(16, 2 *...]
where the time goes in v4:
time: 120 us
  Pallas kernels  119 us (99%)
    pallas_call x1, Pallas kernels, on_device(): pl.pallas_call(fused_kernel, out_shape=(shape(2, 128, 256), shape(16, 2 *...  117 us

profile of v4, /device:TPU:2, one launch (start us, length us, event | category | flops | bytes accessed | tf_op | source)
XLA Modules:
  0.0 119.7 jit_solution(8298426123338266905)
XLA Ops:
  0.6 117.0 %fused.1 = (bf16[2,128,256]{2,1,0:T(8,128)(2,1)}, bf16[16,5120]{1,0:T(8,128)(2,1)}, bf16[320,256]{1,0:T(8,128)(2,1)}, bf16[320,256]{1,0:T(8,128)(2,1)}, bf16[320,256]{1,0:T(8,128)(2,1)}) custom-call(bf16[16,5120]{1,0:T(8,128)(2,1)} %bitcast.3, bf16[320,256]{1,0:T(8,128)(2,1)} %wq.1, bf16[320,256]{1,0:T(8,128)(2,1)} %wk.1, bf16[320,256]{1,0:T(8,128)(2,1)} %wv.1, ...), custom_call_target="tpu_custom_call" | custom-call | tf_op jit(solution)/shard_map/fused/pallas_call | solution.py:641
  117.6 2.0 %hand_over.1 = (bf16[2,128,256]{2,1,0:T(8,128)(2,1)}, bf16[16,5120]{1,0:T(8,128)(2,1)}, bf16[320,256]{1,0:T(8,128)(2,1)}, bf16[320,256]{1,0:T(8,128)(2,1)}, bf16[320,256]{1,0:T(8,128)(2,1)}) custom-call(bf16[2,128,256]{2,1,0:T(8,128)(2,1)} %get-tuple-element.15.refs_0_, bf16[16,5120]{1,0:T(8,128)(2,1)} %get-tuple-element.16.refs_1_, ...), custom_call_target="tpu_custom_call" | custom-call | tf_op jit(solution)/shard_map/hand_over/pallas_call | solution.py:674

commit v5 on v4

--- a/solution.py
+++ b/solution.py
@@ -284,7 +284,7 @@
             kept[pair, m] = jnp.where(v == 0, left, right)
             return carry
 
-        lax.fori_loop(1, 3, one, 0)
+        lax.fori_loop(1, 3, one, 0, unroll=True)
         go(p_cp(2 * pair, 1))
         go(p_cp(2 * pair + 1, 1))
         lax.fori_loop(0, 1, one, 0)
@@ -350,7 +350,7 @@
             acc[:, qs] = jnp.zeros((128, width), F32)
         else:
             start = (stat[0:1, qs], stat[1:2, qs])
-        top, total = lax.fori_loop(2 * kp, 2 * kp + 2, step, start)
+        top, total = lax.fori_loop(2 * kp, 2 * kp + 2, step, start, unroll=True)
         stat[0:1, qs] = top
         stat[1:2, qs] = total
 
@@ -491,7 +491,7 @@
             TG[cam : cam + n, :, :, lanes(i * 640, 640)] = total.reshape(n, 8, 16, 640)
             return carry
 
-        lax.fori_loop(0, 4, some, 0)
+        lax.fori_loop(0, 4, some, 0, unroll=True)
 
     def t_z_cp(d, s, cam):
         return rcopy(

time: 120 us -> 118 us (0.983)
  Pallas kernels: 119 us -> 117 us
    pallas_call x1, Pallas kernels: 117 us -> 115 us  [on_device(): pl.pallas_call(fused_kernel, out_shape=(shape(2, 128, 256), shape(16, 2 *...]
where the time goes in v5:
time: 118 us
  Pallas kernels  117 us (99%)
    pallas_call x1, Pallas kernels, on_device(): pl.pallas_call(fused_kernel, out_shape=(shape(2, 128, 256), shape(16, 2 *...  115 us

profile of v5, /device:TPU:2, one launch (start us, length us, event | category | flops | bytes accessed | tf_op | source)
XLA Modules:
  0.0 118.2 jit_solution(9448508552412024040)
XLA Ops:
  0.6 115.4 %fused.1 = (bf16[2,128,256]{2,1,0:T(8,128)(2,1)}, bf16[16,5120]{1,0:T(8,128)(2,1)}, bf16[320,256]{1,0:T(8,128)(2,1)}, bf16[320,256]{1,0:T(8,128)(2,1)}, bf16[320,256]{1,0:T(8,128)(2,1)}) custom-call(bf16[16,5120]{1,0:T(8,128)(2,1)} %bitcast.3, bf16[320,256]{1,0:T(8,128)(2,1)} %wq.1, bf16[320,256]{1,0:T(8,128)(2,1)} %wk.1, bf16[320,256]{1,0:T(8,128)(2,1)} %wv.1, ...), custom_call_target="tpu_custom_call" | custom-call | tf_op jit(solution)/shard_map/fused/pallas_call | solution.py:641
  116.1 2.0 %hand_over.1 = (bf16[2,128,256]{2,1,0:T(8,128)(2,1)}, bf16[16,5120]{1,0:T(8,128)(2,1)}, bf16[320,256]{1,0:T(8,128)(2,1)}, bf16[320,256]{1,0:T(8,128)(2,1)}, bf16[320,256]{1,0:T(8,128)(2,1)}) custom-call(bf16[2,128,256]{2,1,0:T(8,128)(2,1)} %get-tuple-element.15.refs_0_, bf16[16,5120]{1,0:T(8,128)(2,1)} %get-tuple-element.16.refs_1_, ...), custom_call_target="tpu_custom_call" | custom-call | tf_op jit(solution)/shard_map/hand_over/pallas_call | solution.py:674
